TPU v7x, 128 devices: a whole 4x4x4 slice. The times are simulated.
128 devices in a mesh: dp: 16 (over z, x), tile: 8 (over y, core).
Axes of the slice: x: 4, y: 4, z: 4, core: 2. Of those that a mesh axis runs over, the one named last changes fastest.
Arguments:
- frames: bfloat16 [64, 8, 64, 256], P('dp', 'tile'), may hold values from -6 to 6
- kernels: bfloat16 [64, 9, 256, 256], P('dp'), may hold values from -0.125 to 0.125
- experts: int32 [64, 8, 4], P('dp', 'tile'), may hold values from 0 to 63, as said below
- counts: int32 [64, 8], P('dp', 'tile'), may hold values from 2 to 4
- gate_weights: float32 [64, 8, 4], P('dp', 'tile'), may hold values from 0.25 to 1
- cotangent: bfloat16 [64, 8, 64, 256], P('dp', 'tile'), may hold values from -6 to 6
Outputs:
- frames_out: bfloat16 [64, 8, 64, 256], P('dp', 'tile')
- input_grad: bfloat16 [64, 8, 64, 256], P('dp', 'tile')
- gate_grad: float32 [64, 8, 4], P('dp', 'tile')
- kernel_grad: float32 [64, 9, 256, 256], P('dp', None, None, 'tile')
Inputs may be any that keep to these rules, and one draw needn't show every extreme that they name: A tile's 4 experts have distinct values of id // 4. Among the 4 tiles of one device (frames d * 4 to (d + 1) * 4 - 1 at one tile index), each value of id // 4 is named by at most 2 tiles, by exactly 2 for some, and all its slots there name the same id. A tile uses its first counts slots; later slots are ignored.
All inputs are finite; a program needn't handle non-finite values.
Results may differ from a plain program's by a relative error of at most 0.005.
Values may be sent and summed in bfloat16 or wider, within the bound.
No kernel may reach another device: no remote copies, remote signals or barrier semaphores. Data moves between devices by JAX's collectives and lax.ppermute only.
A program may use at most 256 MiB of HBM per device.

v0:
```python
import jax
import jax.numpy as jnp
from jax import lax
from jax.sharding import PartitionSpec as P

CAP = 2


highest = lax.Precision.HIGHEST


def padded(x, sides, width):
    for axis, dim in sides:
        count, length = (lax.axis_size(axis), x.shape[dim])
        up = [(i, (i + 1) % count) for i in range(count - 1)]
        down = [(j, i) for i, j in up]
        last = lax.slice_in_dim(x, length - width, length, axis=dim)
        initial = lax.slice_in_dim(x, 0, width, axis=dim)
        before = lax.ppermute(last, axis, up)
        after = lax.ppermute(initial, axis, down)
        x = jnp.concatenate([before, x, after], axis=dim)
    return x


def convolve(window, kernel_weight):
    number_of_rows = window.shape[0] - 2
    columns = window.shape[1]
    widened = jnp.pad(window, ((0, 0), (1, 1), (0, 0)))
    total = jnp.zeros((number_of_rows * columns, kernel_weight.shape[2]), jnp.float32)
    for row_off in range(3):
        for col_off in range(3):
            patch = widened[
                row_off : row_off + number_of_rows, col_off : col_off + columns
            ].reshape(number_of_rows * columns, -1)
            total = total + jnp.dot(
                patch, kernel_weight[3 * row_off + col_off], preferred_element_type=jnp.float32
            )
    return total.reshape(number_of_rows, columns, -1)


def transpose_conv(grad_out, kernel_weight):
    number_of_rows = grad_out.shape[0]
    columns = grad_out.shape[1]
    widened = jnp.pad(grad_out, ((2, 2), (1, 1), (0, 0)))
    total = jnp.zeros(((number_of_rows + 2) * columns, kernel_weight.shape[1]), jnp.float32)
    for row_off in range(3):
        for col_off in range(3):
            patch = widened[
                2 - row_off : 4 - row_off + number_of_rows, 2 - col_off : 2 - col_off + columns
            ].reshape((number_of_rows + 2) * columns, -1)
            total = total + lax.dot_general(
                patch,
                kernel_weight[3 * row_off + col_off],
                (((1,), (1,)), ((), ())),
                preferred_element_type=jnp.float32,
            )
    return total.reshape(number_of_rows + 2, columns, -1)


def activation(pre):
    squash = jax.nn.sigmoid(pre)
    return (pre * squash, squash * (1.0 + pre * (1.0 - squash)))


def owner_forward(inputs, expert_pick, item_filled, kernels):
    sources, capacity = (inputs.shape[0], inputs.shape[1])
    flat_inputs = inputs.reshape((sources * capacity,) + inputs.shape[2:])
    flat_pick = jnp.repeat(expert_pick, capacity)
    flat_flag = item_filled.reshape(-1)
    out_shape = (inputs.shape[2] - 2,) + inputs.shape[3:]

    def single(item):
        window, pick_one, flag_item = item
        return lax.cond(
            flag_item,
            lambda: convolve(window, kernels[pick_one]).astype(jnp.bfloat16),
            lambda: jnp.zeros(out_shape, jnp.bfloat16),
        )

    computed = lax.map(single, (flat_inputs, flat_pick, flat_flag))
    return computed.reshape((sources, capacity) + out_shape)


def owner_transpose(grad_items, expert_pick, item_filled, kernels):
    sources, capacity = (grad_items.shape[0], grad_items.shape[1])
    flat_grads = grad_items.reshape((sources * capacity,) + grad_items.shape[2:])
    flat_pick = jnp.repeat(expert_pick, capacity)
    flat_flag = item_filled.reshape(-1)
    out_shape = (grad_items.shape[2] + 2, grad_items.shape[3], kernels.shape[2])

    def single(item):
        grad_one, pick_one, flag_item = item
        return lax.cond(
            flag_item,
            lambda: transpose_conv(grad_one, kernels[pick_one]).astype(jnp.bfloat16),
            lambda: jnp.zeros(out_shape, jnp.bfloat16),
        )

    computed = lax.map(single, (flat_grads, flat_pick, flat_flag))
    return computed.reshape((sources, capacity) + out_shape)


def owner_kernel_terms(inputs, grad_items, expert_pick, local_count):
    sources, capacity = (inputs.shape[0], inputs.shape[1])
    number_of_rows = grad_items.shape[2]
    columns = grad_items.shape[3]
    channels = inputs.shape[4]
    widened = jnp.pad(inputs, ((0, 0), (0, 0), (0, 0), (1, 1), (0, 0)))
    flat_grad = grad_items.reshape(sources, capacity * number_of_rows * columns, channels)
    pieces = []
    for row_off in range(3):
        for col_off in range(3):
            patch = widened[
                :, :, row_off : row_off + number_of_rows, col_off : col_off + columns
            ].reshape(sources, capacity * number_of_rows * columns, channels)
            pieces.append(
                lax.dot_general(
                    patch,
                    flat_grad,
                    (((1,), (1,)), ((0,), (0,))),
                    preferred_element_type=jnp.float32,
                )
            )
    tap_terms = jnp.stack(pieces, axis=1)
    onehot = (expert_pick[:, None] == jnp.arange(local_count)[None, :]).astype(jnp.float32)
    return jnp.einsum("oe,otij->etij", onehot, tap_terms, precision=highest)


def shards(frames, kernels, experts, counts, gate_weights, cotangent):
    owners_count = lax.axis_size("dp")
    specialist_within_tile = kernels.shape[0]
    capacity = CAP
    with_rim = padded(frames, (("tile", 1),), 1)
    center = frames.astype(jnp.float32)
    upstream = cotangent.astype(jnp.float32)
    chosen = experts[:, 0]
    number_of_frames, slot_count = chosen.shape
    active = jnp.arange(slot_count)[None, :] < counts[:, 0][:, None]
    gate_rows = gate_weights[:, 0]
    owner_of = chosen // specialist_within_tile
    local_of = chosen % specialist_within_tile
    named_owner = owner_of[:, :, None] == jnp.arange(owners_count)[None, None, :]
    slot_hit = named_owner & active[:, :, None]
    hit_float = slot_hit.astype(jnp.float32)
    wanted = jnp.any(slot_hit, axis=1)
    position = jnp.cumsum(wanted.astype(jnp.int32), axis=0) - 1
    slot_map = wanted.T[:, None, :] & (
        position.T[:, None, :] == jnp.arange(capacity)[None, :, None]
    )
    slot_float = slot_map.astype(jnp.float32)
    filled = jnp.any(slot_map, axis=2)
    local_request = jnp.max(jnp.where(slot_hit, local_of[:, :, None], -1), axis=(0, 1))
    request = jnp.concatenate([local_request[:, None], filled.astype(jnp.int32)], axis=1)
    asked = lax.all_to_all(request, "dp", split_axis=0, concat_axis=0, tiled=True)
    expert_pick = jnp.maximum(asked[:, 0], 0)
    item_filled = asked[:, 1:] > 0
    tile_gate = jnp.einsum("fso,fs->fo", hit_float, gate_rows, precision=highest)
    weight = jnp.einsum("ocf,fo->oc", slot_float, tile_gate, precision=highest)
    outgoing = jnp.einsum(
        "ocf,frwk->ocrwk",
        slot_map.astype(jnp.bfloat16),
        with_rim,
        preferred_element_type=jnp.float32,
    ).astype(jnp.bfloat16)
    inputs = lax.all_to_all(outgoing, "dp", split_axis=0, concat_axis=0, tiled=True)
    computed = owner_forward(inputs, expert_pick, item_filled, kernels)
    returned = lax.all_to_all(computed, "dp", split_axis=0, concat_axis=0, tiled=True)
    activated, slope = activation(returned.astype(jnp.float32))
    combined = weight[:, :, None, None, None] * activated
    result = center + jnp.einsum("ocf,ocrwk->frwk", slot_float, combined, precision=highest)
    per_item = jnp.einsum("frwk,ocrwk->ocf", upstream, activated, precision=highest)
    selected_entries = jnp.sum(slot_float * per_item, axis=1)
    gate_grad = jnp.einsum("fso,of->fs", hit_float, selected_entries, precision=highest)
    upstream_item = jnp.einsum("ocf,frwk->ocrwk", slot_float, upstream, precision=highest)
    grad_pre = (upstream_item * weight[:, :, None, None, None] * slope).astype(jnp.bfloat16)
    received = lax.all_to_all(grad_pre, "dp", split_axis=0, concat_axis=0, tiled=True)
    back_items = owner_transpose(received, expert_pick, item_filled, kernels)
    kernel_grad = owner_kernel_terms(inputs, received, expert_pick, specialist_within_tile)
    arrived = lax.all_to_all(back_items, "dp", split_axis=0, concat_axis=0, tiled=True)
    rim_sum = jnp.einsum(
        "ocf,ocrwk->frwk", slot_float, arrived.astype(jnp.float32), precision=highest
    )
    edge_rows = jnp.stack([rim_sum[:, 0], rim_sum[:, -1]], axis=1)
    outer_rows = padded(edge_rows.astype(jnp.bfloat16), (("tile", 1),), 1).astype(edge_rows.dtype)
    inner_rows = rim_sum[:, 1:-1]
    inner_rows = inner_rows.at[:, 0].add(outer_rows[:, 0])
    inner_rows = inner_rows.at[:, -1].add(outer_rows[:, 3])
    input_grad = (upstream + inner_rows).astype(jnp.bfloat16)
    kernel_part = lax.psum_scatter(kernel_grad, "tile", scatter_dimension=3, tiled=True)
    return (result.astype(jnp.bfloat16), input_grad, gate_grad[:, None, :], kernel_part)


def solution(mesh):
    return jax.shard_map(
        shards,
        mesh=mesh,
        in_specs=(
            P("dp", "tile", None, None),
            P("dp", None, None, None),
            P("dp", "tile", None),
            P("dp", "tile"),
            P("dp", "tile", None),
            P("dp", "tile", None, None),
        ),
        out_specs=(
            P("dp", "tile", None, None),
            P("dp", "tile", None, None),
            P("dp", "tile", None),
            P("dp", None, None, "tile"),
        ),
        check_vma=False,
    )
```

profile of v0, /device:TPU:16, one launch (start us, length us, event | category | flops | bytes accessed | tf_op | source)
XLA Modules:
  0.0 1156.5 jit_solution(9968861870256880118)
XLA Ops:
  14.9 7.9 all-to-all-start
  24.1 2.8 copy.154
  27.0 3.3 all-to-all-done
  30.2 4.0 all-to-all-start.1
  35.0 48.6 %all-to-all-done.1 = bf16[16,2,3,64,256]{4,3,2,1,0:T(8,128)(2,1)S(1)} async-done(((bf16[16,2,3,64,256]{4,3,2,1,0:T(8,128)(2,1)}), bf16[16,2,3,64,256]{4,3,2,1,0:T(8,128)(2,1)S(1)}, u32[]{:S(2)}, u32[]{:S(2)}) %all-to-all-start.1) | async-done | bytes 3145760 | tf_op jit(solution)/shard_map/all_to_all | solution.py:165
  83.7 193.1 %while.24 = (s32[]{:T(128)}, bf16[32,1,64,256]{3,2,1,0:T(8,128)(2,1)}, pred[32]{0:T(512)(128)(4,1)}, bf16[32,3,64,256]{3,2,1,0:T(8,128)(2,1)S(1)}, bf16[4,9,256,...) while((s32[]{:T(128)}, bf16[32,1,64,256]{3,2,1,0:T(8,128)(2,1)}, pred[32]{0:T(512)(128)(4,1)}, ...), condition=%wide.region_7.8_spmd.clone, body=%wide.region_4.7_spmd.clone.sunk | while | flops 75644928 | bytes 3214118 | solution.py:80
  106.3 12.3 %conditional.6 = (bf16[1,1,64,256]{3,2,1,0:T(8,128)(2,1)S(1)}) conditional(s32[]{:T(128)} %bitcast.275, () %tuple.110, (bf16[32,3,64,256]{3,2,1,0:T(8,128)(2,1)S(1)}, s32[]{:T(128)}, s32[16]{0:T(128)S(1)}, bf16[4,9,256,256]{3,2,1,0:T(8,128)(2,1)}) %tuple.111), branch_computations={%region_5.5_spmd, %region_6.6_spmd} | conditional | flops 75644928 | bytes 3147942 | solution.py:74
  134.1 12.3 %conditional.6 = (bf16[1,1,64,256]{3,2,1,0:T(8,128)(2,1)S(1)}) conditional(s32[]{:T(128)} %bitcast.275, () %tuple.110, (bf16[32,3,64,256]{3,2,1,0:T(8,128)(2,1)S(1)}, s32[]{:T(128)}, s32[16]{0:T(128)S(1)}, bf16[4,9,256,256]{3,2,1,0:T(8,128)(2,1)}) %tuple.111), branch_computations={%region_5.5_spmd, %region_6.6_spmd} | conditional | flops 75644928 | bytes 3147942 | solution.py:74
  148.9 12.3 %conditional.6 = (bf16[1,1,64,256]{3,2,1,0:T(8,128)(2,1)S(1)}) conditional(s32[]{:T(128)} %bitcast.275, () %tuple.110, (bf16[32,3,64,256]{3,2,1,0:T(8,128)(2,1)S(1)}, s32[]{:T(128)}, s32[16]{0:T(128)S(1)}, bf16[4,9,256,256]{3,2,1,0:T(8,128)(2,1)}) %tuple.111), branch_computations={%region_5.5_spmd, %region_6.6_spmd} | conditional | flops 75644928 | bytes 3147942 | solution.py:74
  163.8 12.3 %conditional.6 = (bf16[1,1,64,256]{3,2,1,0:T(8,128)(2,1)S(1)}) conditional(s32[]{:T(128)} %bitcast.275, () %tuple.110, (bf16[32,3,64,256]{3,2,1,0:T(8,128)(2,1)S(1)}, s32[]{:T(128)}, s32[16]{0:T(128)S(1)}, bf16[4,9,256,256]{3,2,1,0:T(8,128)(2,1)}) %tuple.111), branch_computations={%region_5.5_spmd, %region_6.6_spmd} | conditional | flops 75644928 | bytes 3147942 | solution.py:74
  178.6 12.3 %conditional.6 = (bf16[1,1,64,256]{3,2,1,0:T(8,128)(2,1)S(1)}) conditional(s32[]{:T(128)} %bitcast.275, () %tuple.110, (bf16[32,3,64,256]{3,2,1,0:T(8,128)(2,1)S(1)}, s32[]{:T(128)}, s32[16]{0:T(128)S(1)}, bf16[4,9,256,256]{3,2,1,0:T(8,128)(2,1)}) %tuple.111), branch_computations={%region_5.5_spmd, %region_6.6_spmd} | conditional | flops 75644928 | bytes 3147942 | solution.py:74
  193.4 12.3 %conditional.6 = (bf16[1,1,64,256]{3,2,1,0:T(8,128)(2,1)S(1)}) conditional(s32[]{:T(128)} %bitcast.275, () %tuple.110, (bf16[32,3,64,256]{3,2,1,0:T(8,128)(2,1)S(1)}, s32[]{:T(128)}, s32[16]{0:T(128)S(1)}, bf16[4,9,256,256]{3,2,1,0:T(8,128)(2,1)}) %tuple.111), branch_computations={%region_5.5_spmd, %region_6.6_spmd} | conditional | flops 75644928 | bytes 3147942 | solution.py:74
  210.9 12.3 %conditional.6 = (bf16[1,1,64,256]{3,2,1,0:T(8,128)(2,1)S(1)}) conditional(s32[]{:T(128)} %bitcast.275, () %tuple.110, (bf16[32,3,64,256]{3,2,1,0:T(8,128)(2,1)S(1)}, s32[]{:T(128)}, s32[16]{0:T(128)S(1)}, bf16[4,9,256,256]{3,2,1,0:T(8,128)(2,1)}) %tuple.111), branch_computations={%region_5.5_spmd, %region_6.6_spmd} | conditional | flops 75644928 | bytes 3147942 | solution.py:74
  225.7 12.3 %conditional.6 = (bf16[1,1,64,256]{3,2,1,0:T(8,128)(2,1)S(1)}) conditional(s32[]{:T(128)} %bitcast.275, () %tuple.110, (bf16[32,3,64,256]{3,2,1,0:T(8,128)(2,1)S(1)}, s32[]{:T(128)}, s32[16]{0:T(128)S(1)}, bf16[4,9,256,256]{3,2,1,0:T(8,128)(2,1)}) %tuple.111), branch_computations={%region_5.5_spmd, %region_6.6_spmd} | conditional | flops 75644928 | bytes 3147942 | solution.py:74
  240.5 12.3 %conditional.6 = (bf16[1,1,64,256]{3,2,1,0:T(8,128)(2,1)S(1)}) conditional(s32[]{:T(128)} %bitcast.275, () %tuple.110, (bf16[32,3,64,256]{3,2,1,0:T(8,128)(2,1)S(1)}, s32[]{:T(128)}, s32[16]{0:T(128)S(1)}, bf16[4,9,256,256]{3,2,1,0:T(8,128)(2,1)}) %tuple.111), branch_computations={%region_5.5_spmd, %region_6.6_spmd} | conditional | flops 75644928 | bytes 3147942 | solution.py:74
  276.7 245.5 %all-to-all-start.2 = ((bf16[16,2,1,64,256]{4,3,1,2,0:T(8,128)(2,1)}), bf16[16,2,1,64,256]{4,3,1,2,0:T(8,128)(2,1)}, u32[]{:S(2)}, u32[]{:S(2)}) async-start(bf16[16,2,1,64,256]{4,3,1,2,0:T(8,128)(2,1)} %bitcast.309), calls=%async_computation.2 | async-start | bytes 2097152 | tf_op jit(solution)/shard_map/all_to_all | solution.py:167
  522.4 13.2 %all-to-all-done.2 = bf16[16,2,1,64,256]{4,3,1,2,0:T(8,128)(2,1)} async-done(((bf16[16,2,1,64,256]{4,3,1,2,0:T(8,128)(2,1)}), bf16[16,2,1,64,256]{4,3,1,2,0:T(8,128)(2,1)}, u32[]{:S(2)}, u32[]{:S(2)}) %all-to-all-start.2) | async-done | bytes 1048608 | tf_op jit(solution)/shard_map/all_to_all | solution.py:167
  535.6 2.7 fusion.53
  539.7 3.7 all-to-all-start.3
  543.6 6.7 pad_slice_fusion.15
  550.3 6.3 all-to-all-done.3
  556.7 4.0 bitcast_dynamic-update-slice_fusion.8
  560.7 2.7 bitcast_dynamic-update-slice_fusion.7
  563.5 2.7 bitcast_dynamic-update-slice_fusion.6
  566.2 2.7 bitcast_dynamic-update-slice_fusion.5
  568.9 2.7 bitcast_dynamic-update-slice_fusion.4
  571.6 2.7 bitcast_dynamic-update-slice_fusion.3
  574.3 2.7 bitcast_dynamic-update-slice_fusion.2
  577.1 2.7 bitcast_dynamic-update-slice_fusion.1
  579.8 2.8 bitcast_dynamic-update-slice_fusion
  582.6 37.4 %copy.209 = f32[16,9,256,256]{2,0,1,3:T(8,128)} copy(f32[16,9,256,256]{3,2,0,1:T(8,128)} %bitcast_dynamic-update-slice_fusion) | data formatting | bytes 75497472 | tf_op jit(solution)/shard_map/stack | solution.py:124
  620.0 20.8 %fusion.100 = f32[4,9,256,256]{2,0,1,3:T(4,128)} fusion(f32[16,9,256,256]{2,0,1,3:T(8,128)} %copy.209, s32[16]{0:T(128)S(1)} %get-tuple-element.449), kind=kOutput, calls=%fused_computation.172 | convolution fusion | flops 452984896 | bytes 47185984 | tf_op jit(solution)/shard_map/oe,otij->etij/dot_general | solution.py:126
  640.8 198.9 %while.25 = (s32[]{:T(128)}, bf16[32,3,64,256]{3,2,1,0:T(8,128)(2,1)}, pred[32]{0:T(512)(128)(4,1)}, bf16[32,1,64,256]{3,2,1,0:T(8,128)(2,1)S(1)}, bf16[4,9,256,...) while((s32[]{:T(128)}, bf16[32,3,64,256]{3,2,1,0:T(8,128)(2,1)}, pred[32]{0:T(512)(128)(4,1)}, ...), condition=%wide.region_11.12_spmd.clone, body=%wide.region_8.11_spmd.clone.sunk | while | flops 226934784 | bytes 6489374 | solution.py:99
  663.4 13.0 %conditional.7 = (bf16[1,3,64,256]{3,2,1,0:T(8,128)(2,1)S(1)}) conditional(s32[]{:T(128)} %bitcast.276, () %tuple.113, (bf16[32,1,64,256]{3,2,1,0:T(8,128)(2,1)S(1)}, s32[]{:T(128)}, s32[16]{0:T(128)S(1)}, bf16[4,9,256,256]{3,2,1,0:T(8,128)(2,1)}) %tuple.114), branch_computations={%region_9.9_spmd, %region_10.10_spmd} | conditional | flops 226934784 | bytes 6292126 | solution.py:93
  691.8 13.0 %conditional.7 = (bf16[1,3,64,256]{3,2,1,0:T(8,128)(2,1)S(1)}) conditional(s32[]{:T(128)} %bitcast.276, () %tuple.113, (bf16[32,1,64,256]{3,2,1,0:T(8,128)(2,1)S(1)}, s32[]{:T(128)}, s32[16]{0:T(128)S(1)}, bf16[4,9,256,256]{3,2,1,0:T(8,128)(2,1)}) %tuple.114), branch_computations={%region_9.9_spmd, %region_10.10_spmd} | conditional | flops 226934784 | bytes 6292126 | solution.py:93
  707.4 13.0 %conditional.7 = (bf16[1,3,64,256]{3,2,1,0:T(8,128)(2,1)S(1)}) conditional(s32[]{:T(128)} %bitcast.276, () %tuple.113, (bf16[32,1,64,256]{3,2,1,0:T(8,128)(2,1)S(1)}, s32[]{:T(128)}, s32[16]{0:T(128)S(1)}, bf16[4,9,256,256]{3,2,1,0:T(8,128)(2,1)}) %tuple.114), branch_computations={%region_9.9_spmd, %region_10.10_spmd} | conditional | flops 226934784 | bytes 6292126 | solution.py:93
  722.9 13.0 %conditional.7 = (bf16[1,3,64,256]{3,2,1,0:T(8,128)(2,1)S(1)}) conditional(s32[]{:T(128)} %bitcast.276, () %tuple.113, (bf16[32,1,64,256]{3,2,1,0:T(8,128)(2,1)S(1)}, s32[]{:T(128)}, s32[16]{0:T(128)S(1)}, bf16[4,9,256,256]{3,2,1,0:T(8,128)(2,1)}) %tuple.114), branch_computations={%region_9.9_spmd, %region_10.10_spmd} | conditional | flops 226934784 | bytes 6292126 | solution.py:93
  738.4 13.0 %conditional.7 = (bf16[1,3,64,256]{3,2,1,0:T(8,128)(2,1)S(1)}) conditional(s32[]{:T(128)} %bitcast.276, () %tuple.113, (bf16[32,1,64,256]{3,2,1,0:T(8,128)(2,1)S(1)}, s32[]{:T(128)}, s32[16]{0:T(128)S(1)}, bf16[4,9,256,256]{3,2,1,0:T(8,128)(2,1)}) %tuple.114), branch_computations={%region_9.9_spmd, %region_10.10_spmd} | conditional | flops 226934784 | bytes 6292126 | solution.py:93
  753.9 13.0 %conditional.7 = (bf16[1,3,64,256]{3,2,1,0:T(8,128)(2,1)S(1)}) conditional(s32[]{:T(128)} %bitcast.276, () %tuple.113, (bf16[32,1,64,256]{3,2,1,0:T(8,128)(2,1)S(1)}, s32[]{:T(128)}, s32[16]{0:T(128)S(1)}, bf16[4,9,256,256]{3,2,1,0:T(8,128)(2,1)}) %tuple.114), branch_computations={%region_9.9_spmd, %region_10.10_spmd} | conditional | flops 226934784 | bytes 6292126 | solution.py:93
  772.0 13.0 %conditional.7 = (bf16[1,3,64,256]{3,2,1,0:T(8,128)(2,1)S(1)}) conditional(s32[]{:T(128)} %bitcast.276, () %tuple.113, (bf16[32,1,64,256]{3,2,1,0:T(8,128)(2,1)S(1)}, s32[]{:T(128)}, s32[16]{0:T(128)S(1)}, bf16[4,9,256,256]{3,2,1,0:T(8,128)(2,1)}) %tuple.114), branch_computations={%region_9.9_spmd, %region_10.10_spmd} | conditional | flops 226934784 | bytes 6292126 | solution.py:93
  787.5 13.0 %conditional.7 = (bf16[1,3,64,256]{3,2,1,0:T(8,128)(2,1)S(1)}) conditional(s32[]{:T(128)} %bitcast.276, () %tuple.113, (bf16[32,1,64,256]{3,2,1,0:T(8,128)(2,1)S(1)}, s32[]{:T(128)}, s32[16]{0:T(128)S(1)}, bf16[4,9,256,256]{3,2,1,0:T(8,128)(2,1)}) %tuple.114), branch_computations={%region_9.9_spmd, %region_10.10_spmd} | conditional | flops 226934784 | bytes 6292126 | solution.py:93
  803.0 13.0 %conditional.7 = (bf16[1,3,64,256]{3,2,1,0:T(8,128)(2,1)S(1)}) conditional(s32[]{:T(128)} %bitcast.276, () %tuple.113, (bf16[32,1,64,256]{3,2,1,0:T(8,128)(2,1)S(1)}, s32[]{:T(128)}, s32[16]{0:T(128)S(1)}, bf16[4,9,256,256]{3,2,1,0:T(8,128)(2,1)}) %tuple.114), branch_computations={%region_9.9_spmd, %region_10.10_spmd} | conditional | flops 226934784 | bytes 6292126 | solution.py:93
  839.8 6.9 copy.162
  846.7 261.2 %all-to-all-start.4 = ((bf16[16,2,3,64,256]{4,1,3,2,0:T(2,128)(2,1)}), bf16[16,2,3,64,256]{4,1,3,2,0:T(2,128)(2,1)S(1)}, u32[]{:S(2)}, u32[]{:S(2)}) async-start(bf16[16,2,3,64,256]{4,1,3,2,0:T(2,128)(2,1)} %copy.162), calls=%async_computation.4 | async-start | bytes 6291456 | tf_op jit(solution)/shard_map/all_to_all | solution.py:179
  1109.1 2.9 fusion.68
  1112.7 5.0 fusion.77
  1117.7 18.1 %all-to-all-done.4 = bf16[16,2,3,64,256]{4,1,3,2,0:T(2,128)(2,1)S(1)} async-done(((bf16[16,2,3,64,256]{4,1,3,2,0:T(2,128)(2,1)}), bf16[16,2,3,64,256]{4,1,3,2,0:T(2,128)(2,1)S(1)}, u32[]{:S(2)}, u32[]{:S(2)}) %all-to-all-start.4) | async-done | bytes 3145760 | tf_op jit(solution)/shard_map/all_to_all | solution.py:179
  1143.0 3.2 collective-permute-done.2
  (529 shorter events, 339.0 us)
Async XLA Ops:
  7.2 515.1 %copy-start = (f32[4,1,4]{2,1,0:T(1,128)S(1)}, f32[4,1,4]{2,1,0:T(1,128)}, u32[]{:S(2)}) copy-start(f32[4,1,4]{2,1,0:T(1,128)} %param.22) | copy-start | bytes 196
  8.2 14.6 %collective-permute-start.1 = (bf16[4,1,64,256]{3,0,2,1:T(4,128)(2,1)S(1)}, bf16[4,1,64,256]{3,0,2,1:T(4,128)(2,1)S(1)}, u32[]{:S(2)}, u32[]{:S(2)}) collective-permute-start(bf16[4,1,64,256]{3,0,2,1:T(4,128)(2,1)S(1)} %copy.147), channel_id=1, source_target_pairs={{1,0},{2,1},{3,2},{4,3},{5,4},{6,5},{7,6},{9,8},{10,9},{11,10},{12... | collective-permute-start | bytes 393224 | tf_op jit(solution)/shard_map/ppermute | solution.py:20
  10.1 12.6 %collective-permute-start = (bf16[4,1,64,256]{3,0,2,1:T(4,128)(2,1)S(1)}, bf16[4,1,64,256]{3,0,2,1:T(4,128)(2,1)S(1)}, u32[]{:S(2)}, u32[]{:S(2)}) collective-permute-start(bf16[4,1,64,256]{3,0,2,1:T(4,128)(2,1)S(1)} %copy.147), channel_id=1, source_target_pairs={{0,1},{1,2},{2,3},{3,4},{4,5},{5,6},{6,7},{8,9},{9,10},{10,11},{11... | collective-permute-start | bytes 393224 | tf_op jit(solution)/shard_map/ppermute | solution.py:19
  14.9 15.4 %all-to-all-start = ((s32[16,1,3]{2,1,0:T(1,128)}), s32[16,1,3]{2,1,0:T(1,128)S(1)}, u32[]{:S(2)}, u32[]{:S(2)}) async-start(s32[16,1,3]{2,1,0:T(1,128)} %copy.148), calls=%async_computation | async-start | bytes 16384 | tf_op jit(solution)/shard_map/all_to_all | solution.py:154
  30.2 53.4 %all-to-all-start.1 = ((bf16[16,2,3,64,256]{4,3,2,1,0:T(8,128)(2,1)}), bf16[16,2,3,64,256]{4,3,2,1,0:T(8,128)(2,1)S(1)}, u32[]{:S(2)}, u32[]{:S(2)}) async-start(bf16[16,2,3,64,256]{4,3,2,1,0:T(8,128)(2,1)} %copy.154), calls=%async_computation.1 | async-start | bytes 6291456 | tf_op jit(solution)/shard_map/all_to_all | solution.py:165
  83.7 452.0 %copy-start.10 = (bf16[4,1,64,256]{3,2,1,0:T(8,128)(2,1)S(1)}, bf16[4,1,64,256]{3,2,1,0:T(8,128)(2,1)}, u32[]{:S(2)}) copy-start(bf16[4,1,64,256]{3,2,1,0:T(8,128)(2,1)} %param.23) | copy-start | bytes 393220
  276.7 261.6 %copy-start.2 = (bf16[32,3,64,256]{3,2,1,0:T(8,128)(2,1)}, bf16[32,3,64,256]{3,2,1,0:T(8,128)(2,1)S(1)}, u32[]{:S(2)}) copy-start(bf16[32,3,64,256]{3,2,1,0:T(8,128)(2,1)S(1)} %get-tuple-element.429) | copy-start | bytes 9437188
  276.7 258.9 %all-to-all-start.2 = ((bf16[16,2,1,64,256]{4,3,1,2,0:T(8,128)(2,1)}), bf16[16,2,1,64,256]{4,3,1,2,0:T(8,128)(2,1)}, u32[]{:S(2)}, u32[]{:S(2)}) async-start(bf16[16,2,1,64,256]{4,3,1,2,0:T(8,128)(2,1)} %bitcast.309), calls=%async_computation.2 | async-start | bytes 2097152 | tf_op jit(solution)/shard_map/all_to_all | solution.py:167
  539.7 17.0 %all-to-all-start.3 = ((bf16[16,2,1,64,256]{4,3,1,2,0:T(8,128)(2,1)}), bf16[16,2,1,64,256]{4,3,1,2,0:T(8,128)(2,1)S(1)}, u32[]{:S(2)}, u32[]{:S(2)}) async-start(bf16[16,2,1,64,256]{4,3,1,2,0:T(8,128)(2,1)} %copy.160), calls=%async_computation.3 | async-start | bytes 2097152 | tf_op jit(solution)/shard_map/all_to_all | solution.py:176
  543.4 603.6 %all-reduce.6.cloned.1.call-start = ((), (), s32[]{:S(2)}) async-start(), calls=%async_computation.5 | async-start | bytes 18874368
  556.7 4.0 copy-start.8
  560.7 2.8 copy-start.7
  563.5 2.7 copy-start.6
  566.2 2.7 copy-start.5
  568.9 2.7 copy-start.4
  571.6 2.8 copy-start.3
  846.6 261.2 %copy-start.11 = (u32[128]{0:T(128)S(1)}, u32[128]{0:T(128)}, u32[]{:S(2)}) copy-start(u32[128]{0:T(128)} %constant.160) | copy-start | bytes 1540
  846.7 262.4 %copy-start.9 = (bf16[4,1,64,256]{3,2,1,0:T(8,128)(2,1)S(1)}, bf16[4,1,64,256]{3,2,1,0:T(8,128)(2,1)}, u32[]{:S(2)}) copy-start(bf16[4,1,64,256]{3,2,1,0:T(8,128)(2,1)} %param.18) | copy-start | bytes 393220
  846.7 289.2 %all-to-all-start.4 = ((bf16[16,2,3,64,256]{4,1,3,2,0:T(2,128)(2,1)}), bf16[16,2,3,64,256]{4,1,3,2,0:T(2,128)(2,1)S(1)}, u32[]{:S(2)}, u32[]{:S(2)}) async-start(bf16[16,2,3,64,256]{4,1,3,2,0:T(2,128)(2,1)} %copy.162), calls=%async_computation.4 | async-start | bytes 6291456 | tf_op jit(solution)/shard_map/all_to_all | solution.py:179
  1135.8 13.9 %copy-start.1 = (f32[4,1,4]{2,1,0:T(1,128)S(1)}, f32[4,1,4]{2,1,0:T(1,128)}, u32[]{:S(2)}) copy-start(f32[4,1,4]{2,1,0:T(1,128)} %param.22) | copy-start | bytes 196
  1137.9 5.1 collective-permute-start.3
  1139.8 6.3 collective-permute-start.2
Sparse Core Ops, SparseCore 0:
  641.0 109.0 all-reduce.5
where the time goes:
time: 1170 us; the launch traced here: 1160 us
  starting transfers between devices  531 us (45%)
  matrix products  238 us (20%)
  local copies, waits for them, and re-layouts  200 us (17%)
  waiting for transfers between devices  92.8 us (8%)
  loops' own time  77.8 us (7%)
  between operations  14.9 us (1%)
    all_to_all x1, starting transfers between devices, shards(): lax.all_to_all(back_items, 'dp', split_axis=0, concat_axis=0, tiled=True)  261 us
    all_to_all x1, starting transfers between devices, shards(): lax.all_to_all(computed, 'dp', split_axis=0, concat_axis=0, tiled=True)  245 us
    dynamic_slice x82, local copies, waits for them, and re-layouts, owner_forward(): computed = lax.map(single, (flat_inputs, flat_pick, flat_flag))  92.6 us
    dot_general x81, matrix products, transpose_conv(): lax.dot_general(patch, kernel_weight[3 * row_off + col_off], (((1,), (1,)...  90.8 us
    dot_general x81, matrix products, convolve(): jnp.dot(patch, kernel_weight[3 * row_off + col_off], preferred_element_ty...  85.8 us
    all_to_all x1, waiting for transfers between devices, shards(): lax.all_to_all(outgoing, 'dp', split_axis=0, concat_axis=0, tiled=True)  48.6 us
    another operation x1, local copies, waits for them, and re-layouts, owner_kernel_terms(): tap_terms = jnp.stack(pieces, axis=1)  37.4 us
    dot_general x9, matrix products, owner_kernel_terms(): lax.dot_general(patch, flat_grad, (((1,), (1,)), ((0,), (0,))), preferred...  25.9 us
  transfers between devices with their start and end apart: 10, of which 6 were waited for; matrix products, arithmetic and copies ran while one was open for 17% of the time, Pallas kernels for 0%

commit v1 on v0

v1 whole, which is shorter than its diff:
```python
import functools

import jax
import jax.numpy as jnp
from jax import lax
from jax.experimental import pallas as pl
from jax.experimental.pallas import tpu as pltpu
from jax.sharding import PartitionSpec as P

DP = 16
TILES = 8
CAP = 2
ITEMS = DP * CAP
FRAMES = 4
SLOTS = 4
LOCAL = 4
W = 64
C = 256
PACK = 4
ROWS = PACK * W
MAX_GROUPS = 12
MIB = 2**20

SMEM = pl.BlockSpec(memory_space=pltpu.SMEM)
VMEM = pl.BlockSpec(memory_space=pltpu.VMEM)


def route_kernel(experts, counts, gates, meta, slot_frame, item_slot, used):
    def clear(o, carry):
        used[o] = 0
        slot_frame[2 * o] = -1
        slot_frame[2 * o + 1] = -1
        for k in range(8):
            meta[o, k] = 0.0
        return carry

    lax.fori_loop(0, DP, clear, 0)
    for f in range(FRAMES):
        for j in range(SLOTS):
            item_slot[f * SLOTS + j] = -1

            @pl.when(j < counts[f])
            def _():
                e = experts[f, j]
                o = e // LOCAL
                c = used[o]
                used[o] = c + 1
                slot_frame[CAP * o + c] = f
                item_slot[f * SLOTS + j] = CAP * o + c
                meta[o, 0] = (e - o * LOCAL).astype(jnp.float32)
                meta[o, 1 + c] = 1.0
                meta[o, 3 + c] = gates[f, j]


def route(experts, counts, gates):
    return pl.pallas_call(
        route_kernel,
        out_shape=(
            jax.ShapeDtypeStruct((DP, 8), jnp.float32),
            jax.ShapeDtypeStruct((ITEMS,), jnp.int32),
            jax.ShapeDtypeStruct((FRAMES * SLOTS,), jnp.int32),
        ),
        in_specs=[SMEM] * 3,
        out_specs=(SMEM,) * 3,
        scratch_shapes=[pltpu.SMEM((DP,), jnp.int32)],
        name="route",
    )(experts, counts, gates)


def pack_kernel(slot_frame, frames, above, below, cotangent, out):
    step = pl.program_id(0)
    for k in range(8):
        f = slot_frame[step * 8 + k]

        @pl.when(f >= 0)
        def _():
            out[k, 0] = above[f]
            out[k, 1] = frames[f]
            out[k, 2] = below[f]
            out[k, 3] = cotangent[f]


def pack(slot_frame, frames, above, below, cotangent):
    whole = pl.BlockSpec((FRAMES, W, C), lambda i, s: (0, 0, 0))
    return pl.pallas_call(
        pack_kernel,
        grid_spec=pltpu.PrefetchScalarGridSpec(
            num_scalar_prefetch=1,
            grid=(ITEMS // 8,),
            in_specs=[whole] * 4,
            out_specs=pl.BlockSpec((8, 4, W, C), lambda i, s: (i, 0, 0, 0)),
        ),
        out_shape=jax.ShapeDtypeStruct((ITEMS, 4, W, C), jnp.bfloat16),
        compiler_params=pltpu.CompilerParams(vmem_limit_bytes=24 * MIB),
        name="pack",
    )(slot_frame, frames, above, below, cotangent)


def list_kernel(meta, order, scale, group_expert, groups):
    def clear(p, carry):
        order[p] = -1
        scale[p] = 0.0
        return carry

    lax.fori_loop(0, MAX_GROUPS * PACK, clear, 0)
    first = jnp.int32(0)
    for e in range(LOCAL):

        def take(s, place, e=e):
            here = meta[s, 0] == float(e)
            for c in range(CAP):
                hit = here & (meta[s, 1 + c] > 0.5)

                @pl.when(hit)
                def _():
                    order[place] = CAP * s + c
                    scale[place] = meta[s, 3 + c]

                place = place + jnp.where(hit, 1, 0)
            return place

        last = lax.fori_loop(0, DP, take, first * PACK)
        size = (last - first * PACK + PACK - 1) // PACK

        def name(g, carry, e=e):
            group_expert[g] = e
            return carry

        lax.fori_loop(first, first + size, name, 0)
        first = first + size
    groups[0] = first


def make_list(meta):
    return pl.pallas_call(
        list_kernel,
        out_shape=(
            jax.ShapeDtypeStruct((MAX_GROUPS * PACK,), jnp.int32),
            jax.ShapeDtypeStruct((MAX_GROUPS * PACK,), jnp.float32),
            jax.ShapeDtypeStruct((MAX_GROUPS,), jnp.int32),
            jax.ShapeDtypeStruct((1,), jnp.int32),
        ),
        in_specs=[SMEM],
        out_specs=(SMEM,) * 4,
        name="item_list",
    )(meta)


def slope_of(pre):
    squash = jax.nn.sigmoid(pre)
    return squash * (1.0 + pre * (1.0 - squash))


def earlier(x, column):
    return jnp.where(column == 0, 0.0, pltpu.roll(x, 1, 0))


def later(x, column):
    return jnp.where(column == W - 1, 0.0, pltpu.roll(x, x.shape[0] - 1, 0))


def owner_kernel(
    order, scale, group_expert, groups, items, weights, flipped, back, grads, window, upstream, wide
):
    column = lax.broadcasted_iota(jnp.int32, (ROWS, C), 0) % W

    def group(g, carry):
        e = group_expert[g]
        for k in range(PACK):
            rows = pl.ds(k * W, W)
            item = order[g * PACK + k]
            there = item >= 0
            item = jnp.maximum(item, 0)

            @pl.when(there)
            def _():
                for r in range(3):
                    window[rows, r * C : (r + 1) * C] = items[item, r]
                upstream[rows, :] = items[item, 3].astype(jnp.float32) * scale[g * PACK + k]

            @pl.when(jnp.logical_not(there))
            def _():
                window[rows, :] = jnp.zeros((W, 3 * C), jnp.bfloat16)
                upstream[rows, :] = jnp.zeros((W, C), jnp.float32)

        patch = window[...]
        taps = [
            jnp.dot(patch, weights[e, :, b].reshape(3 * C, C), preferred_element_type=jnp.float32)
            for b in range(3)
        ]
        pre = (earlier(taps[0], column) + taps[1] + later(taps[2], column)).astype(jnp.bfloat16)
        grad = (upstream[...] * slope_of(pre.astype(jnp.float32))).astype(jnp.bfloat16)
        grads[g] = grad
        exact = grad.astype(jnp.float32)
        wide[:, 0:C] = later(exact, column).astype(jnp.bfloat16)
        wide[:, C : 2 * C] = grad
        wide[:, 2 * C : 3 * C] = earlier(exact, column).astype(jnp.bfloat16)
        rim = jnp.dot(wide[...], flipped[e], preferred_element_type=jnp.float32).astype(jnp.bfloat16)
        for k in range(PACK):
            item = order[g * PACK + k]

            @pl.when(item >= 0)
            def _():
                here = jnp.maximum(item, 0)
                back[here, 0] = pre[k * W : (k + 1) * W]
                for r in range(3):
                    back[here, 1 + r] = rim[k * W : (k + 1) * W, r * C : (r + 1) * C]

        return carry

    lax.fori_loop(0, groups[0], group, 0)


def owner(order, scale, group_expert, groups, items, weights, flipped):
    return pl.pallas_call(
        owner_kernel,
        out_shape=(
            jax.ShapeDtypeStruct((ITEMS, 4, W, C), jnp.bfloat16),
            jax.ShapeDtypeStruct((MAX_GROUPS, ROWS, C), jnp.bfloat16),
        ),
        in_specs=[SMEM] * 4 + [VMEM] * 3,
        out_specs=(VMEM, VMEM),
        scratch_shapes=[
            pltpu.VMEM((ROWS, 3 * C), jnp.bfloat16),
            pltpu.VMEM((ROWS, C), jnp.float32),
            pltpu.VMEM((ROWS, 3 * C), jnp.bfloat16),
        ],
        compiler_params=pltpu.CompilerParams(vmem_limit_bytes=48 * MIB),
        cost_estimate=pl.CostEstimate(
            flops=24 * 151_000_000, bytes_accessed=20_000_000, transcendentals=500_000
        ),
        name="owner",
    )(order, scale, group_expert, groups, items, weights, flipped)


def terms_kernel(order, group_expert, groups, items, grads, total, window, wide):
    column = lax.broadcasted_iota(jnp.int32, (ROWS, C), 0) % W
    total[...] = jnp.zeros_like(total)

    def group(g, carry):
        e = group_expert[g]
        for k in range(PACK):
            rows = pl.ds(k * W, W)
            item = order[g * PACK + k]

            @pl.when(item >= 0)
            def _():
                for r in range(3):
                    window[rows, r * C : (r + 1) * C] = items[jnp.maximum(item, 0), r]

            @pl.when(item < 0)
            def _():
                window[rows, :] = jnp.zeros((W, 3 * C), jnp.bfloat16)

        grad = grads[g]
        exact = grad.astype(jnp.float32)
        shifted = [later(exact, column), exact, earlier(exact, column)]
        patch = window[...]
        for b in range(3):
            part = jnp.dot(
                shifted[b].T.astype(jnp.bfloat16), patch, preferred_element_type=jnp.float32
            )
            for a in range(3):
                total[:, e, a, b] += part[:, a * C : (a + 1) * C].reshape(TILES, C // TILES, C)
        return carry

    lax.fori_loop(0, groups[0], group, 0)


def terms(order, group_expert, groups, items, grads):
    return pl.pallas_call(
        terms_kernel,
        out_shape=jax.ShapeDtypeStruct((TILES, LOCAL, 3, 3, C // TILES, C), jnp.float32),
        in_specs=[SMEM] * 3 + [VMEM] * 2,
        out_specs=VMEM,
        scratch_shapes=[
            pltpu.VMEM((ROWS, 3 * C), jnp.bfloat16),
            pltpu.VMEM((ROWS, 3 * C), jnp.bfloat16),
        ],
        compiler_params=pltpu.CompilerParams(vmem_limit_bytes=48 * MIB),
        cost_estimate=pl.CostEstimate(
            flops=24 * 75_500_000, bytes_accessed=15_000_000, transcendentals=0
        ),
        name="terms",
    )(order, group_expert, groups, items, grads)


def combine_kernel(item_slot, gates, got, frames, cotangent, out, inner, edges, gate_grad):
    for f in range(FRAMES):
        upstream = cotangent[f].astype(jnp.float32)
        out_acc = frames[f].astype(jnp.float32)
        rim = [jnp.zeros((W, C), jnp.float32) for _ in range(3)]
        for j in range(SLOTS):
            slot = item_slot[f * SLOTS + j]
            there = slot >= 0
            slot = jnp.maximum(slot, 0)
            block = jnp.where(there, got[slot], jnp.zeros((4, W, C), jnp.bfloat16)).astype(
                jnp.float32
            )
            activated = block[0] * jax.nn.sigmoid(block[0])
            out_acc = out_acc + gates[f, j] * activated
            gate_grad[f, j] = jnp.sum(upstream * activated)
            for r in range(3):
                rim[r] = rim[r] + block[1 + r]
        out[f] = out_acc.astype(jnp.bfloat16)
        inner[f] = upstream + rim[1]
        edges[0, f] = rim[0].astype(jnp.bfloat16)
        edges[1, f] = rim[2].astype(jnp.bfloat16)


def combine(item_slot, gates, got, frames, cotangent):
    return pl.pallas_call(
        combine_kernel,
        out_shape=(
            jax.ShapeDtypeStruct((FRAMES, W, C), jnp.bfloat16),
            jax.ShapeDtypeStruct((FRAMES, W, C), jnp.float32),
            jax.ShapeDtypeStruct((2, FRAMES, W, C), jnp.bfloat16),
            jax.ShapeDtypeStruct((FRAMES, SLOTS), jnp.float32),
        ),
        in_specs=[SMEM] * 2 + [VMEM] * 3,
        out_specs=(VMEM, VMEM, VMEM, SMEM),
        compiler_params=pltpu.CompilerParams(vmem_limit_bytes=24 * MIB),
        name="combine",
    )(item_slot, gates, got, frames, cotangent)


UP = [(i, i + 1) for i in range(TILES - 1)]
DOWN = [(i + 1, i) for i in range(TILES - 1)]


def shards(frames, kernels, experts, counts, gate_weights, cotangent):
    frames = frames[:, 0]
    cotangent = cotangent[:, 0]
    gates = gate_weights[:, 0]
    above = lax.ppermute(frames, "tile", UP)
    below = lax.ppermute(frames, "tile", DOWN)
    meta, slot_frame, item_slot = route(experts[:, 0], counts[:, 0], gates)
    asked = lax.all_to_all(meta, "dp", split_axis=0, concat_axis=0, tiled=True)
    outgoing = pack(slot_frame, frames, above, below, cotangent)
    items = lax.all_to_all(outgoing, "dp", split_axis=0, concat_axis=0, tiled=True)
    weights = kernels.reshape(LOCAL, 3, 3, C, C)
    flipped = weights.transpose(0, 2, 4, 1, 3).reshape(LOCAL, 3 * C, 3 * C)
    order, scale, group_expert, groups = make_list(asked)
    back, grads = owner(order, scale, group_expert, groups, items, weights, flipped)
    got = lax.all_to_all(back, "dp", split_axis=0, concat_axis=0, tiled=True)
    total = terms(order, group_expert, groups, items, grads)
    part = lax.psum_scatter(
        total.reshape(TILES, LOCAL * 9 * (C // TILES), C), "tile", scatter_dimension=0, tiled=True
    )
    kernel_grad = part.reshape(LOCAL, 9, C // TILES, C).transpose(0, 1, 3, 2)
    out, inner, edges, gate_grad = combine(item_slot, gates, got, frames, cotangent)
    from_below = lax.ppermute(edges[0], "tile", DOWN)
    from_above = lax.ppermute(edges[1], "tile", UP)
    input_grad = (
        inner + from_below.astype(jnp.float32) + from_above.astype(jnp.float32)
    ).astype(jnp.bfloat16)
    return (out[:, None], input_grad[:, None], gate_grad[:, None], kernel_grad)


def solution(mesh):
    return jax.shard_map(
        shards,
        mesh=mesh,
        in_specs=(
            P("dp", "tile", None, None),
            P("dp", None, None, None),
            P("dp", "tile", None),
            P("dp", "tile"),
            P("dp", "tile", None),
            P("dp", "tile", None, None),
        ),
        out_specs=(
            P("dp", "tile", None, None),
            P("dp", "tile", None, None),
            P("dp", "tile", None),
            P("dp", None, None, "tile"),
        ),
        check_vma=False,
    )
```

time: 1170 us -> 204 us (0.17); the launches traced: 1160 us -> 203 us
  starting transfers between devices: 531 us -> 21.8 us
  matrix products: 238 us -> 0 us
  local copies, waits for them, and re-layouts: 200 us -> 32.2 us
  loops' own time: 77.8 us -> 0 us
  blocking collectives: 0 us -> 53 us
  waiting for transfers between devices: 92.8 us -> 45.6 us
  Pallas kernels: 0 us -> 35.4 us
    all_to_all x4 -> x1, starting transfers between devices: 518 us -> 7.89 us  [shards(): asked = lax.all_to_all(meta, 'dp', split_axis=0, concat_axis=0, tiled=True)]
    dot_general x179 -> x0, matrix products: 238 us -> none  [the longest x81 90.8 us: transpose_conv(): lax.dot_general(patch, kernel_weight[3 * row_off + col_off], (((1,), (1,)...]
    dynamic_slice x82 -> x0, local copies, waits for them, and re-layouts: 92.6 us -> none  [owner_forward(): computed = lax.map(single, (flat_inputs, flat_pick, flat_flag))]
    another operation x66 -> x0, loops' own time: 77.8 us -> none  [the longest x1 21.1 us: owner_transpose(): computed = lax.map(single, (flat_grads, flat_pick, flat_flag))]
    all_to_all x0 -> x1, blocking collectives: none -> 53 us  [shards(): got = lax.all_to_all(back, 'dp', split_axis=0, concat_axis=0, tiled=True)]
    dynamic_update_slice x64 -> x0, local copies, waits for them, and re-layouts: 40.7 us -> none  [the longest x32 20.7 us: owner_transpose(): computed = lax.map(single, (flat_grads, flat_pick, flat_flag))]
    all_to_all x4 -> x1, waiting for transfers between devices: 40.9 us -> 2.06 us  [shards(): asked = lax.all_to_all(meta, 'dp', split_axis=0, concat_axis=0, tiled=True)]
    another operation x1 -> x0, local copies, waits for them, and re-layouts: 37.4 us -> none  [owner_kernel_terms(): tap_terms = jnp.stack(pieces, axis=1)]
  transfers between devices with their start and end apart: 10 -> 7, of which waited for: 6 -> 4; matrix products, arithmetic and copies ran while one was open for 17% -> 12% of each run, Pallas kernels for 0% -> 4%
where the time goes in v1:
time: 204 us; the launch traced here: 203 us
  blocking collectives  53 us (26%)
  waiting for transfers between devices  45.6 us (22%)
  Pallas kernels  35.4 us (17%)
  local copies, waits for them, and re-layouts  32.2 us (16%)
  starting transfers between devices  21.8 us (11%)
  between operations  14.2 us (7%)
    all_to_all x1, blocking collectives, shards(): got = lax.all_to_all(back, 'dp', split_axis=0, concat_axis=0, tiled=True)  53 us
    all_to_all x1, waiting for transfers between devices, shards(): lax.all_to_all(outgoing, 'dp', split_axis=0, concat_axis=0, tiled=True)  38.4 us
    pallas_call x1, Pallas kernels, owner(): pl.pallas_call(owner_kernel, out_shape=(jax.ShapeDtypeStruct((ITEMS, 4, W...  16.1 us
    reshape x1, local copies, waits for them, and re-layouts, shards(): flipped = weights.transpose(0, 2, 4, 1, 3).reshape(LOCAL, 3 * C, 3 * C)  13 us
    pallas_call x1, Pallas kernels, terms(): pl.pallas_call(terms_kernel, out_shape=jax.ShapeDtypeStruct((TILES, LOCAL...  11.9 us
    transpose x1, local copies, waits for them, and re-layouts, shards(): flipped = weights.transpose(0, 2, 4, 1, 3).reshape(LOCAL, 3 * C, 3 * C)  10.1 us
    unnamed x28, local copies, waits for them, and re-layouts  9 us
    all_to_all x1, starting transfers between devices, shards(): asked = lax.all_to_all(meta, 'dp', split_axis=0, concat_axis=0, tiled=True)  7.89 us
  transfers between devices with their start and end apart: 7, of which 4 were waited for; matrix products, arithmetic and copies ran while one was open for 12% of the time, Pallas kernels for 4%

profile of v1, /device:TPU:16, one launch (start us, length us, event | category | flops | bytes accessed | tf_op | source)
XLA Modules:
  0.0 203.0 jit_solution(16386781790177307120)
XLA Ops:
  7.2 1.9 collective-permute-start.1
  9.1 2.4 %collective-permute-start = (bf16[4,64,256]{2,1,0:T(8,128)(2,1)}, bf16[4,64,256]{2,1,0:T(8,128)(2,1)S(1)}, u32[]{:S(2)}, u32[]{:S(2)}) collective-permute-start(bf16[4,64,256]{2,1,0:T(8,128)(2,1)} %bitcast.31), channel_id=1, source_target_pairs={{0,1},{1,2},{2,3},{3,4},{4,5},{5,6},{6,7},{8,9},{9,10},{10,11},{11... | collective-permute-start | bytes 393224 | tf_op jit(solution)/shard_map/ppermute | solution.py:335
  11.5 1.8 route.1
  13.3 7.9 %all-to-all-start = ((f32[16,1,8]{2,1,0:T(1,128)}), f32[16,1,8]{2,1,0:T(1,128)S(1)}, u32[]{:S(2)}, u32[]{:S(2)}) async-start(f32[16,1,8]{2,1,0:T(1,128)} %bitcast.42), calls=%async_computation | async-start | bytes 16384 | tf_op jit(solution)/shard_map/all_to_all | solution.py:338
  21.2 0.0 collective-permute-done.1.below
  21.3 0.0 collective-permute-done.above
  21.3 0.0 copy-start.2
  21.3 0.9 copy-done.2
  22.2 0.0 copy-start.4
  22.2 0.9 copy-done.4
  23.1 0.0 copy-start.11
  23.1 0.7 copy-done.11
  23.7 0.9 pack.1
  24.7 0.0 copy-start
  24.7 2.0 copy-done
  26.7 2.1 %all-to-all-done = f32[16,1,8]{2,1,0:T(1,128)S(1)} async-done(((f32[16,1,8]{2,1,0:T(1,128)}), f32[16,1,8]{2,1,0:T(1,128)S(1)}, u32[]{:S(2)}, u32[]{:S(2)}) %all-to-all-start) | async-done | bytes 544 | tf_op jit(solution)/shard_map/all_to_all | solution.py:338
  28.7 0.0 copy-start.13
  28.7 0.6 copy-done.13
  29.3 5.2 %all-to-all-start.1 = ((bf16[32,4,64,256]{3,2,1,0:T(8,128)(2,1)}), bf16[32,4,64,256]{3,2,1,0:T(8,128)(2,1)}, u32[]{:S(2)}, u32[]{:S(2)}) async-start(bf16[32,4,64,256]{3,2,1,0:T(8,128)(2,1)} %copy-done), calls=%async_computation.1 | async-start | bytes 8388608 | tf_op jit(solution)/shard_map/all_to_all | solution.py:340
  34.6 0.0 reduce-scatter.2.cloned.1.call-start
  34.6 10.1 %copy.26 = bf16[4,3,256,3,256]{4,3,2,1,0:T(4,128)(2,1)} copy(bf16[4,3,256,3,256]{2,4,1,3,0:T(8,128)(2,1)} %bitcast.39) | data formatting | bytes 9437184 | tf_op jit(solution)/shard_map/transpose | solution.py:342
  44.8 13.0 %reshape.23.flipped = bf16[4,768,768]{2,1,0:T(8,128)(2,1)} reshape(bf16[4,3,256,3,256]{4,3,2,1,0:T(4,128)(2,1)} %copy.26) | data formatting | bytes 9437184 | tf_op jit(solution)/shard_map/reshape | solution.py:342
  57.8 2.7 %item_list.1 = (s32[48]{0:T(128)}, f32[48]{0:T(128)}, s32[12]{0:T(128)}, s32[1]{0:T(128)}) custom-call(f32[16,8]{1,0:T(8,128)} %bitcast.41), custom_call_target="tpu_custom_call" | custom-call | tf_op jit(solution)/shard_map/item_list/pallas_call | solution.py:135
  60.5 38.4 %all-to-all-done.1.items = bf16[32,4,64,256]{3,2,1,0:T(8,128)(2,1)} async-done(((bf16[32,4,64,256]{3,2,1,0:T(8,128)(2,1)}), bf16[32,4,64,256]{3,2,1,0:T(8,128)(2,1)}, u32[]{:S(2)}, u32[]{:S(2)}) %all-to-all-start.1) | async-done | bytes 4194336 | tf_op jit(solution)/shard_map/all_to_all | solution.py:340
  98.9 0.7 copy-done.7
  99.6 0.7 copy-done.8
  100.3 0.7 copy-done.12
  100.9 16.1 %owner.1 = (bf16[32,4,64,256]{3,2,1,0:T(8,128)(2,1)S(1)}, bf16[12,256,256]{2,1,0:T(8,128)(2,1)S(1)}) custom-call(s32[48]{0:T(128)S(1)} %copy-done.7, f32[48]{0:T(128)S(1)} %copy-done.12, s32[12]{0:T(128)S(1)} %copy-done.8, s32[1]{0:T(128)} %get-tuple-element.22.groups, bf16[32,4,64,256]{3,2,1,0:T(8,128)(2,1)} %all-to-all-done.1.items, ...), custom_call_target="tpu_custom_call" | custom-call | flops 3624000000 | bytes 20000000 | tf_op jit(solution)/shard_map/owner/pallas_call | solution.py:215
  117.0 0.0 copy-start.1
  117.0 2.0 copy-done.1
  119.0 0.0 copy-done.9
  119.0 11.9 %terms.1 = f32[8,4,3,3,32,256]{5,4,3,2,1,0:T(8,128)} custom-call(s32[48]{0:T(128)S(1)} %copy-done.7, s32[12]{0:T(128)S(1)} %copy-done.9, s32[1]{0:T(128)} %get-tuple-element.22.groups, bf16[32,4,64,256]{3,2,1,0:T(8,128)(2,1)} %all-to-all-done.1.items, bf16[12,256,256]{2,1,0:T(8,128)(2,1)S(1)} %get-tuple-element.29.grads), custom_call_target="tpu_custom_call" | custom-call | flops 1812000000 | bytes 15000000 | tf_op jit(solution)/shard_map/terms/pallas_call | solution.py:271
  130.9 0.0 reduce-scatter.2.cloned.1.call-update
  130.9 0.0 copy-start.3
  131.0 0.0 copy-start.5
  131.0 0.0 copy-start.6
  131.0 0.0 copy-start.10
  131.0 53.0 %all_to_all.21.got = bf16[32,4,64,256]{3,2,1,0:T(8,128)(2,1)S(1)} all-to-all(bf16[32,4,64,256]{3,2,1,0:T(8,128)(2,1)} %copy-done.1), channel_id=1, replica_groups=mesh['dp'=16,'tile'=8] {'dp'}, dimensions={0} | all-to-all | bytes 8388608 | tf_op jit(solution)/shard_map/all_to_all | solution.py:345
  184.0 0.0 copy-done.3
  184.0 0.0 copy-done.5
  184.0 0.0 copy-done.6
  184.0 0.0 copy-done.10
  184.0 1.9 combine.1
  186.0 1.9 collective-permute-start.2
  187.9 2.4 %collective-permute-start.3 = (bf16[4,64,256]{2,1,0:T(8,128)(2,1)S(1)}, bf16[4,64,256]{2,1,0:T(8,128)(2,1)S(1)}, u32[]{:S(2)}, u32[]{:S(2)}) collective-permute-start(bf16[4,64,256]{2,1,0:T(8,128)(2,1)S(1)} %get-tuple-element.43), channel_id=1, source_target_pairs={{0,1},{1,2},{2,3},{3,4},{4,5},{5,6},{6,7},{8,9},{9,10},{10,11},{11... | collective-permute-start | bytes 393224 | tf_op jit(solution)/shard_map/ppermute | solution.py:353
  190.3 0.1 collective-permute-done.2
  190.4 5.1 %collective-permute-done.3 = bf16[4,64,256]{2,1,0:T(8,128)(2,1)S(1)} collective-permute-done((bf16[4,64,256]{2,1,0:T(8,128)(2,1)S(1)}, bf16[4,64,256]{2,1,0:T(8,128)(2,1)S(1)}, u32[]{:S(2)}, u32[]{:S(2)}) %collective-permute-start.3) | collective-permute-done | bytes 131104 | tf_op jit(solution)/shard_map/ppermute | solution.py:353
  195.5 0.7 fusion
  (6 shorter events, 0.0 us)
Async XLA Ops:
  7.2 14.1 %collective-permute-start.1 = (bf16[4,64,256]{2,1,0:T(8,128)(2,1)}, bf16[4,64,256]{2,1,0:T(8,128)(2,1)S(1)}, u32[]{:S(2)}, u32[]{:S(2)}) collective-permute-start(bf16[4,64,256]{2,1,0:T(8,128)(2,1)} %bitcast.30), channel_id=1, source_target_pairs={{1,0},{2,1},{3,2},{4,3},{5,4},{6,5},{7,6},{9,8},{10,9},{11,10},{12... | collective-permute-start | bytes 393224 | tf_op jit(solution)/shard_map/ppermute | solution.py:336
  9.1 12.2 %collective-permute-start = (bf16[4,64,256]{2,1,0:T(8,128)(2,1)}, bf16[4,64,256]{2,1,0:T(8,128)(2,1)S(1)}, u32[]{:S(2)}, u32[]{:S(2)}) collective-permute-start(bf16[4,64,256]{2,1,0:T(8,128)(2,1)} %bitcast.31), channel_id=1, source_target_pairs={{0,1},{1,2},{2,3},{3,4},{4,5},{5,6},{6,7},{8,9},{9,10},{10,11},{11... | collective-permute-start | bytes 393224 | tf_op jit(solution)/shard_map/ppermute | solution.py:335
  13.3 15.4 %all-to-all-start = ((f32[16,1,8]{2,1,0:T(1,128)}), f32[16,1,8]{2,1,0:T(1,128)S(1)}, u32[]{:S(2)}, u32[]{:S(2)}) async-start(f32[16,1,8]{2,1,0:T(1,128)} %bitcast.42), calls=%async_computation | async-start | bytes 16384 | tf_op jit(solution)/shard_map/all_to_all | solution.py:338
  21.3 0.9 copy-start.2
  22.2 0.9 copy-start.4
  23.1 0.7 copy-start.11
  24.7 2.0 copy-start
  28.7 0.6 copy-start.13
  29.3 69.6 %all-to-all-start.1 = ((bf16[32,4,64,256]{3,2,1,0:T(8,128)(2,1)}), bf16[32,4,64,256]{3,2,1,0:T(8,128)(2,1)}, u32[]{:S(2)}, u32[]{:S(2)}) async-start(bf16[32,4,64,256]{3,2,1,0:T(8,128)(2,1)} %copy-done), calls=%async_computation.1 | async-start | bytes 8388608 | tf_op jit(solution)/shard_map/all_to_all | solution.py:340
  34.6 161.6 %reduce-scatter.2.cloned.1.call-start = ((), (), s32[]{:S(2)}) async-start(), calls=%async_computation.4 | async-start | bytes 10616832 | tf_op jit(solution)/shard_map/reduce_scatter | solution.py:347
  98.9 0.7 copy-start.7
  99.6 0.7 copy-start.8
  100.3 0.7 copy-start.12
  100.9 18.1 %copy-start.9 = (s32[12]{0:T(128)S(1)}, s32[12]{0:T(128)}, u32[]{:S(2)}) copy-start(s32[12]{0:T(128)} %get-tuple-element.21.group_expert) | copy-start | bytes 148
  117.0 2.0 copy-start.1
  130.9 53.1 %copy-start.3 = (bf16[4,1,64,256]{3,2,1,0:T(8,128)(2,1)S(1)}, bf16[4,1,64,256]{3,2,1,0:T(8,128)(2,1)}, u32[]{:S(2)}) copy-start(bf16[4,1,64,256]{3,2,1,0:T(8,128)(2,1)} %param.6) | copy-start | bytes 393220
  131.0 53.1 %copy-start.5 = (bf16[4,1,64,256]{3,2,1,0:T(8,128)(2,1)S(1)}, bf16[4,1,64,256]{3,2,1,0:T(8,128)(2,1)}, u32[]{:S(2)}) copy-start(bf16[4,1,64,256]{3,2,1,0:T(8,128)(2,1)} %param.11) | copy-start | bytes 393220
  131.0 53.1 %copy-start.6 = (f32[4,1,4]{2,1,0:T(1,128)S(1)}, f32[4,1,4]{2,1,0:T(1,128)}, u32[]{:S(2)}) copy-start(f32[4,1,4]{2,1,0:T(1,128)} %param.10) | copy-start | bytes 196
  131.0 53.1 %copy-start.10 = (s32[16]{0:T(128)S(1)}, s32[16]{0:T(128)}, u32[]{:S(2)}) copy-start(s32[16]{0:T(128)} %get-tuple-element.17.item_slot) | copy-start | bytes 196
  186.0 4.4 %collective-permute-start.2 = (bf16[4,64,256]{2,1,0:T(8,128)(2,1)S(1)}, bf16[4,64,256]{2,1,0:T(8,128)(2,1)S(1)}, u32[]{:S(2)}, u32[]{:S(2)}) collective-permute-start(bf16[4,64,256]{2,1,0:T(8,128)(2,1)S(1)} %get-tuple-element.42), channel_id=1, source_target_pairs={{1,0},{2,1},{3,2},{4,3},{5,4},{6,5},{7,6},{9,8},{10,9},{11,10},{12... | collective-permute-start | bytes 393224 | tf_op jit(solution)/shard_map/ppermute | solution.py:352
  187.9 7.6 %collective-permute-start.3 = (bf16[4,64,256]{2,1,0:T(8,128)(2,1)S(1)}, bf16[4,64,256]{2,1,0:T(8,128)(2,1)S(1)}, u32[]{:S(2)}, u32[]{:S(2)}) collective-permute-start(bf16[4,64,256]{2,1,0:T(8,128)(2,1)S(1)} %get-tuple-element.43), channel_id=1, source_target_pairs={{0,1},{1,2},{2,3},{3,4},{4,5},{5,6},{6,7},{8,9},{9,10},{10,11},{11... | collective-permute-start | bytes 393224 | tf_op jit(solution)/shard_map/ppermute | solution.py:353
Sparse Core Ops, SparseCore 0:
  131.1 52.1 reduce-scatter.1

commit v2 on v1

v2 whole, which is shorter than its diff:
```python
import functools

import jax
import jax.numpy as jnp
from jax import lax
from jax.experimental import pallas as pl
from jax.experimental.pallas import tpu as pltpu
from jax.sharding import PartitionSpec as P

DP = 16
TILES = 8
CAP = 2
ITEMS = DP * CAP
FRAMES = 4
SLOTS = 4
LOCAL = 4
W = 64
C = 256
PACK = 4
ROWS = PACK * W
MAX_GROUPS = 7
MIB = 2**20
BLOCKS = W // 16
ITEM_BLOCKS = 4 * BLOCKS
KNOWN = 5

SMEM = pl.BlockSpec(memory_space=pltpu.SMEM)
VMEM = pl.BlockSpec(memory_space=pltpu.VMEM)
HBM = pl.BlockSpec(memory_space=pltpu.HBM)


def route_kernel(experts, counts, gates, frames, cotangent, item_slot, tags, half, used, known):
    for f in range(FRAMES):
        for r, source in ((1, frames), (3, cotangent)):
            half[f, r * BLOCKS : (r + 1) * BLOCKS] = source[f].reshape(BLOCKS, 16, C)

    def clear(o, carry):
        used[o] = 0
        for k in range(KNOWN):
            known[o, k] = 0.0
        return carry

    lax.fori_loop(0, DP, clear, 0)
    for f in range(FRAMES):
        for j in range(SLOTS):
            i = f * SLOTS + j
            item_slot[i] = -1

            @pl.when(j < counts[f])
            def _(f=f, j=j, i=i):
                e = experts[f, j]
                o = e // LOCAL
                place = used[o]
                used[o] = place + 1
                item_slot[i] = CAP * o + place
                known[o, 0] = (e - o * LOCAL).astype(jnp.float32)
                known[o, 1 + place] = 1.0
                known[o, 3 + place] = gates[f, j]

    lane = lax.broadcasted_iota(jnp.int32, (16, C), 1)
    line = lax.broadcasted_iota(jnp.int32, (16, C), 0)
    for o in range(DP):
        values = jnp.zeros((16, C), jnp.float32)
        for k in range(KNOWN):
            values = jnp.where(lane == k, known[o, k], values)
        high = values.astype(jnp.bfloat16).astype(jnp.float32)
        middle = (values - high).astype(jnp.bfloat16).astype(jnp.float32)
        low = values - high - middle
        tags[o] = jnp.where(
            line == 0, high, jnp.where(line == 1, middle, jnp.where(line == 2, low, 0.0))
        ).astype(jnp.bfloat16)


def route(experts, counts, gates, frames, cotangent):
    return pl.pallas_call(
        route_kernel,
        out_shape=(
            jax.ShapeDtypeStruct((FRAMES * SLOTS,), jnp.int32),
            jax.ShapeDtypeStruct((DP, 16, C), jnp.bfloat16),
            jax.ShapeDtypeStruct((FRAMES, ITEM_BLOCKS, 16, C), jnp.bfloat16),
        ),
        in_specs=[SMEM] * 3 + [VMEM] * 2,
        out_specs=(SMEM, VMEM, VMEM),
        scratch_shapes=[pltpu.SMEM((DP,), jnp.int32), pltpu.SMEM((DP, KNOWN), jnp.float32)],
        compiler_params=pltpu.CompilerParams(vmem_limit_bytes=8 * MIB),
        name="route",
    )(experts, counts, gates, frames, cotangent)


def pack_kernel(item_slot, tags, half, above, below, out_0, out_1, tiles, sems, tag_sems):
    def send_tile(i, act):
        slot = item_slot[i]
        for c, target in enumerate((out_0, out_1)):

            @pl.when((slot >= 0) & (slot % CAP == c))
            def _(c=c, target=target):
                copy = pltpu.make_async_copy(
                    tiles.at[i // SLOTS],
                    target.at[jnp.maximum(slot, 0) // CAP, pl.ds(0, ITEM_BLOCKS)],
                    sems.at[i],
                )
                copy.start() if act == "start" else copy.wait()

    def send_tags(o, act):
        copy = pltpu.make_async_copy(tags.at[o], out_0.at[o, ITEM_BLOCKS], tag_sems.at[o])
        copy.start() if act == "start" else copy.wait()

    for o in range(DP):
        send_tags(o, "start")
    for f in range(FRAMES):
        tiles[f] = half[f]
        for r, source in ((0, above), (2, below)):
            tiles[f, r * BLOCKS : (r + 1) * BLOCKS] = source[f].reshape(BLOCKS, 16, C)
        for j in range(SLOTS):
            send_tile(f * SLOTS + j, "start")
    for o in range(DP):
        send_tags(o, "wait")
    for i in range(FRAMES * SLOTS):
        send_tile(i, "wait")


def pack(item_slot, tags, half, above, below):
    return pl.pallas_call(
        pack_kernel,
        out_shape=(
            jax.ShapeDtypeStruct((DP, ITEM_BLOCKS + 1, 16, C), jnp.bfloat16),
            jax.ShapeDtypeStruct((DP, ITEM_BLOCKS, 16, C), jnp.bfloat16),
        ),
        in_specs=[SMEM] + [VMEM] * 4,
        out_specs=(HBM, HBM),
        scratch_shapes=[
            pltpu.VMEM((FRAMES, ITEM_BLOCKS, 16, C), jnp.bfloat16),
            pltpu.SemaphoreType.DMA((FRAMES * SLOTS,)),
            pltpu.SemaphoreType.DMA((DP,)),
        ],
        compiler_params=pltpu.CompilerParams(vmem_limit_bytes=8 * MIB),
        name="pack",
    )(item_slot, tags, half, above, below)


def list_kernel(meta, *refs):
    found, size = refs[4 * CAP :]
    for c in range(CAP):
        order, scale, group_expert, groups = refs[4 * c : 4 * c + 4]

        def clear(p, carry, order=order, scale=scale):
            order[p] = -1
            scale[p] = 0.0
            return carry

        lax.fori_loop(0, MAX_GROUPS * PACK, clear, 0)
        for e in range(LOCAL):
            size[e] = 0

        def source(s, carry, c=c):
            @pl.when(meta[s, 1 + c] > 0.5)
            def _():
                e = meta[s, 0].astype(jnp.int32)
                n = size[e]
                found[e, n] = s
                size[e] = n + 1

            return carry

        lax.fori_loop(0, DP, source, 0)
        first = jnp.int32(0)
        for e in range(LOCAL):

            def copy(n, carry, e=e, c=c, order=order, scale=scale):
                s = found[e, n]
                order[carry + n] = s
                scale[carry + n] = meta[s, 3 + c]
                return carry

            lax.fori_loop(0, size[e], copy, first * PACK)
            last = first + (size[e] + PACK - 1) // PACK

            def name(g, carry, e=e, group_expert=group_expert):
                group_expert[g] = e
                return carry

            lax.fori_loop(first, last, name, 0)
            first = last
        groups[0] = first


def make_lists(meta):
    one = (
        jax.ShapeDtypeStruct((MAX_GROUPS * PACK,), jnp.int32),
        jax.ShapeDtypeStruct((MAX_GROUPS * PACK,), jnp.float32),
        jax.ShapeDtypeStruct((MAX_GROUPS,), jnp.int32),
        jax.ShapeDtypeStruct((1,), jnp.int32),
    )
    made = pl.pallas_call(
        list_kernel,
        out_shape=one * CAP,
        in_specs=[SMEM],
        out_specs=(SMEM,) * (4 * CAP),
        scratch_shapes=[
            pltpu.SMEM((LOCAL, DP), jnp.int32),
            pltpu.SMEM((LOCAL,), jnp.int32),
        ],
        name="item_lists",
    )(meta)
    return [made[4 * c : 4 * c + 4] for c in range(CAP)]


def slope_of(pre):
    squash = jax.nn.sigmoid(pre)
    return squash * (1.0 + pre * (1.0 - squash))


def earlier(x, column):
    return jnp.where(column == 0, 0.0, pltpu.roll(x, 1, 0))


def later(x, column):
    return jnp.where(column == W - 1, 0.0, pltpu.roll(x, x.shape[0] - 1, 0))


def row_of(items, item, r):
    return items[jnp.maximum(item, 0), r * BLOCKS : (r + 1) * BLOCKS].reshape(W, C)


def owner_kernel(place, order, scale, group_expert, groups, items, weights, *refs):
    if place == 0:
        back, pre_out, grads, window, upstream = refs
    else:
        other_pre, back, grads, window, upstream = refs
        pre_out = None
        back[:, 4] = other_pre[...]
    column = lax.broadcasted_iota(jnp.int32, (ROWS, C), 0) % W

    def group(g, carry):
        e = group_expert[g]
        for k in range(PACK):
            rows = pl.ds(k * W, W)
            item = order[g * PACK + k]

            @pl.when(item >= 0)
            def _():
                for r in range(3):
                    window[rows, r * C : (r + 1) * C] = row_of(items, item, r)
                upstream[rows, :] = row_of(items, item, 3).astype(jnp.float32) * scale[g * PACK + k]

            @pl.when(item < 0)
            def _():
                window[rows, :] = jnp.zeros((W, 3 * C), jnp.bfloat16)
                upstream[rows, :] = jnp.zeros((W, C), jnp.float32)

        patch = window[...]
        taps = [
            jnp.dot(patch, weights[e, :, b].reshape(3 * C, C), preferred_element_type=jnp.float32)
            for b in range(3)
        ]
        pre = (earlier(taps[0], column) + taps[1] + later(taps[2], column)).astype(jnp.bfloat16)
        grad = (upstream[...] * slope_of(pre.astype(jnp.float32))).astype(jnp.bfloat16)
        grads[g] = grad
        exact = grad.astype(jnp.float32)
        shifted = [
            later(exact, column).astype(jnp.bfloat16),
            grad,
            earlier(exact, column).astype(jnp.bfloat16),
        ]
        rims = [
            sum(
                lax.dot_general(
                    shifted[b],
                    weights[e, a, b],
                    (((1,), (1,)), ((), ())),
                    preferred_element_type=jnp.float32,
                )
                for b in range(3)
            ).astype(jnp.bfloat16)
            for a in range(3)
        ]
        for k in range(PACK):
            item = order[g * PACK + k]

            @pl.when(item >= 0)
            def _(k=k):
                here = jnp.maximum(item, 0)
                if pre_out is None:
                    back[here, 3] = pre[k * W : (k + 1) * W]
                else:
                    pre_out[here] = pre[k * W : (k + 1) * W]
                for r in range(3):
                    back[here, r] = rims[r][k * W : (k + 1) * W]

        return carry

    lax.fori_loop(0, groups[0], group, 0)


def owner(order, scale, group_expert, groups, items, weights, other_pre=None):
    rows = lambda *n: jax.ShapeDtypeStruct((DP, *n, W, C), jnp.bfloat16)
    more = [] if other_pre is None else [other_pre]
    made = [rows(5)] if more else [rows(3), rows()]
    made.append(jax.ShapeDtypeStruct((MAX_GROUPS, ROWS, C), jnp.bfloat16))
    return pl.pallas_call(
        functools.partial(owner_kernel, len(more)),
        out_shape=made,
        in_specs=[SMEM] * 4 + [VMEM] * (2 + len(more)),
        out_specs=[VMEM] * len(made),
        scratch_shapes=[
            pltpu.VMEM((ROWS, 3 * C), jnp.bfloat16),
            pltpu.VMEM((ROWS, C), jnp.float32),
        ],
        compiler_params=pltpu.CompilerParams(vmem_limit_bytes=16 * MIB),
        cost_estimate=pl.CostEstimate(
            flops=8_000_000_000, bytes_accessed=16_000_000, transcendentals=500_000
        ),
        name="owner",
    )(order, scale, group_expert, groups, items, weights, *more)


def shifted_products(g, order, items, grads, window):
    column = lax.broadcasted_iota(jnp.int32, (ROWS, C), 0) % W
    for k in range(PACK):
        rows = pl.ds(k * W, W)
        item = order[g * PACK + k]

        @pl.when(item >= 0)
        def _():
            for r in range(3):
                window[rows, r * C : (r + 1) * C] = row_of(items, item, r)

        @pl.when(item < 0)
        def _():
            window[rows, :] = jnp.zeros((W, 3 * C), jnp.bfloat16)

    exact = grads[g].astype(jnp.float32)
    patch = window[...]
    for b, x in enumerate((later(exact, column), exact, earlier(exact, column))):
        part = jnp.dot(x.T.astype(jnp.bfloat16), patch, preferred_element_type=jnp.float32)
        for a in range(3):
            yield 3 * a + b, part[:, a * C : (a + 1) * C].reshape(TILES, C // TILES, C)


def groups_before(e, group_expert, groups):
    return lax.fori_loop(
        0, groups[0], lambda g, n: n + jnp.where(group_expert[g] < e, 1, 0), jnp.int32(0)
    )


def terms_kernel(fresh, order, group_expert, groups, items, grads, *refs):
    if fresh:
        total, sums, window, sems = refs
    else:
        before, total, sums, window, sems, so_far, load_sems = refs

    def copy(e):
        return pltpu.make_async_copy(sums.at[e % 2], total.at[:, e], sems.at[e])

    def load(e):
        return pltpu.make_async_copy(before.at[:, e], so_far.at[:, e], load_sems.at[e])

    if not fresh:
        for e in range(LOCAL):
            load(e).start()
    for e in range(LOCAL):
        begin = groups_before(e, group_expert, groups)
        end = groups_before(e + 1, group_expert, groups)
        if e >= 2:
            copy(e - 2).wait()
        if not fresh:
            load(e).wait()

        def group(g, carry, e=e, begin=begin):
            for tap, part in shifted_products(g, order, items, grads, window):

                @pl.when(g == begin)
                def _(tap=tap, part=part):
                    sums[e % 2, :, tap] = part if fresh else so_far[:, e, tap] + part

                @pl.when(g != begin)
                def _(tap=tap, part=part):
                    sums[e % 2, :, tap] += part

            return carry

        lax.fori_loop(begin, end, group, 0)

        @pl.when(end == begin)
        def _(e=e):
            sums[e % 2] = (
                jnp.zeros((TILES, 9, C // TILES, C), jnp.float32) if fresh else so_far[:, e]
            )

        copy(e).start()
    for e in (LOCAL - 2, LOCAL - 1):
        copy(e).wait()


def terms(order, group_expert, groups, items, grads, so_far=None):
    fresh = so_far is None
    made = (TILES, LOCAL, 9, C // TILES, C)
    scratch = [
        pltpu.VMEM((2, TILES, 9, C // TILES, C), jnp.float32),
        pltpu.VMEM((ROWS, 3 * C), jnp.bfloat16),
        pltpu.SemaphoreType.DMA((LOCAL,)),
    ]
    if not fresh:
        scratch += [pltpu.VMEM(made, jnp.float32), pltpu.SemaphoreType.DMA((LOCAL,))]
    return pl.pallas_call(
        functools.partial(terms_kernel, fresh),
        out_shape=jax.ShapeDtypeStruct(made, jnp.float32),
        in_specs=[SMEM] * 3 + [VMEM] * 2 + ([] if fresh else [HBM]),
        out_specs=HBM,
        scratch_shapes=scratch,
        compiler_params=pltpu.CompilerParams(vmem_limit_bytes=48 * MIB),
        cost_estimate=pl.CostEstimate(
            flops=4_000_000_000, bytes_accessed=15_000_000, transcendentals=0
        ),
        name="first_terms" if fresh else "last_terms",
    )(order, group_expert, groups, items, grads, *([] if fresh else [so_far]))


def gathered(item_slot, places, add):
    for f in range(FRAMES):
        for j in range(SLOTS):
            slot = item_slot[f * SLOTS + j]
            for place in places:

                @pl.when((slot >= 0) & (slot % CAP == place))
                def _(f=f, j=j, slot=slot, place=place):
                    add(f, j, jnp.maximum(slot, 0) // CAP, place)


def first_kernel(item_slot, got, cotangent, sums):
    sums[0] = jnp.zeros((FRAMES, W, C), jnp.float32)
    sums[1] = cotangent[...].astype(jnp.float32)
    sums[2] = jnp.zeros((FRAMES, W, C), jnp.float32)

    def add(f, j, o, place):
        for r in range(3):
            sums[r, f] += got[o, r].astype(jnp.float32)

    gathered(item_slot, (0,), add)


def last_kernel(item_slot, gates, got, frames, cotangent, so_far, out, inner, edges, gate_grad, sums, total):
    sums[...] = so_far[...]
    total[...] = frames[...].astype(jnp.float32)
    for f in range(FRAMES):
        for j in range(SLOTS):
            gate_grad[f, j] = 0.0

    def add(f, j, o, place):
        pre = got[o, 4 - place].astype(jnp.float32)
        activated = pre * jax.nn.sigmoid(pre)
        total[f] += gates[f, j] * activated
        gate_grad[f, j] = jnp.sum(cotangent[f].astype(jnp.float32) * activated)
        if place == 1:
            for r in range(3):
                sums[r, f] += got[o, r].astype(jnp.float32)

    gathered(item_slot, (0, 1), add)
    out[...] = total[...].astype(jnp.bfloat16)
    inner[...] = sums[1]
    edges[0] = sums[0].astype(jnp.bfloat16)
    edges[1] = sums[2].astype(jnp.bfloat16)


def combine_first(item_slot, got, cotangent):
    return pl.pallas_call(
        first_kernel,
        out_shape=jax.ShapeDtypeStruct((3, FRAMES, W, C), jnp.float32),
        in_specs=[SMEM] + [VMEM] * 2,
        out_specs=VMEM,
        compiler_params=pltpu.CompilerParams(vmem_limit_bytes=12 * MIB),
        name="combine_first",
    )(item_slot, got, cotangent)


def combine_last(item_slot, gates, got, frames, cotangent, so_far):
    return pl.pallas_call(
        last_kernel,
        out_shape=(
            jax.ShapeDtypeStruct((FRAMES, W, C), jnp.bfloat16),
            jax.ShapeDtypeStruct((FRAMES, W, C), jnp.float32),
            jax.ShapeDtypeStruct((2, FRAMES, W, C), jnp.bfloat16),
            jax.ShapeDtypeStruct((FRAMES, SLOTS), jnp.float32),
        ),
        in_specs=[SMEM] * 2 + [VMEM] * 4,
        out_specs=(VMEM, VMEM, VMEM, SMEM),
        scratch_shapes=[
            pltpu.VMEM((3, FRAMES, W, C), jnp.float32),
            pltpu.VMEM((FRAMES, W, C), jnp.float32),
        ],
        compiler_params=pltpu.CompilerParams(vmem_limit_bytes=12 * MIB),
        name="combine_last",
    )(item_slot, gates, got, frames, cotangent, so_far)


UP = [(i, i + 1) for i in range(TILES - 1)]
DOWN = [(i + 1, i) for i in range(TILES - 1)]


def exchange(x):
    return lax.all_to_all(x, "dp", split_axis=0, concat_axis=0, tiled=True)


def shards(frames, kernels, experts, counts, gate_weights, cotangent):
    frames = frames[:, 0]
    cotangent = cotangent[:, 0]
    gates = gate_weights[:, 0]
    above = lax.ppermute(frames, "tile", UP)
    below = lax.ppermute(frames, "tile", DOWN)
    item_slot, tags, half = route(experts[:, 0], counts[:, 0], gates, frames, cotangent)
    outgoing = list(pack(item_slot, tags, half, above, below))
    items = [exchange(outgoing[0])]
    items[0], outgoing[1] = lax.optimization_barrier((items[0], outgoing[1]))
    items.append(exchange(outgoing[1]))
    meta = jnp.sum(items[0][:, ITEM_BLOCKS, :3, :KNOWN].astype(jnp.float32), axis=1)
    weights = kernels.reshape(LOCAL, 3, 3, C, C)
    lists = make_lists(meta)
    (order_0, scale, *of_groups), (order_1, scale_1, *of_groups_1) = lists
    back, pre, grads = owner(order_0, scale, *of_groups, items[0], weights)
    total = terms(order_0, *of_groups, items[0], grads)
    back, total = lax.optimization_barrier((back, total))
    got = exchange(back)
    rest, grads = owner(order_1, scale_1, *of_groups_1, items[1], weights, pre)
    total = terms(order_1, *of_groups_1, items[1], grads, total)
    total, got = lax.optimization_barrier((total, got))
    part = lax.psum_scatter(
        total.reshape(TILES, LOCAL * 9 * (C // TILES), C), "tile", scatter_dimension=0, tiled=True
    )
    kernel_grad = part.reshape(LOCAL, 9, C // TILES, C).transpose(0, 1, 3, 2)
    so_far = combine_first(item_slot, got, cotangent)
    out, inner, edges, gate_grad = combine_last(
        item_slot, gates, exchange(rest), frames, cotangent, so_far
    )
    from_below = lax.ppermute(edges[0], "tile", DOWN)
    from_above = lax.ppermute(edges[1], "tile", UP)
    input_grad = (
        inner + from_below.astype(jnp.float32) + from_above.astype(jnp.float32)
    ).astype(jnp.bfloat16)
    return (out[:, None], input_grad[:, None], gate_grad[:, None], kernel_grad)


def solution(mesh):
    return jax.shard_map(
        shards,
        mesh=mesh,
        in_specs=(
            P("dp", "tile", None, None),
            P("dp", None, None, None),
            P("dp", "tile", None),
            P("dp", "tile"),
            P("dp", "tile", None),
            P("dp", "tile", None, None),
        ),
        out_specs=(
            P("dp", "tile", None, None),
            P("dp", "tile", None, None),
            P("dp", "tile", None),
            P("dp", None, None, "tile"),
        ),
        check_vma=False,
    )
```

time: 204 us -> 189 us (0.926); the launches traced: 203 us -> 186 us
  local copies, waits for them, and re-layouts: 32.2 us -> 14.5 us
  blocking collectives: 53 us -> 38.3 us
  waiting for transfers between devices: 45.6 us -> 55.8 us
  Pallas kernels: 35.4 us -> 40.2 us
    all_to_all x1, blocking collectives: 53 us -> 38.3 us  [exchange(): return lax.all_to_all(x, 'dp', split_axis=0, concat_axis=0, tiled=True)]
    reshape x1 -> x0, local copies, waits for them, and re-layouts: 13 us -> none  [shards(): flipped = weights.transpose(0, 2, 4, 1, 3).reshape(LOCAL, 3 * C, 3 * C)]
    transpose x1 -> x0, local copies, waits for them, and re-layouts: 10.1 us -> none  [shards(): flipped = weights.transpose(0, 2, 4, 1, 3).reshape(LOCAL, 3 * C, 3 * C)]
    all_to_all x2 -> x3, waiting for transfers between devices: 40.5 us -> 50.5 us  [exchange(): return lax.all_to_all(x, 'dp', split_axis=0, concat_axis=0, tiled=True)]
    unnamed x28 -> x42, local copies, waits for them, and re-layouts: 9 us -> 14.5 us
    pallas_call x6 -> x9, Pallas kernels: 35.4 us -> 40.2 us  [the longest x2 16.9 us: terms(): pl.pallas_call(functools.partial(terms_kernel, fresh), out_shape=jax.Shap...]
    all_to_all x2 -> x3, starting transfers between devices: 13.1 us -> 12 us  [exchange(): return lax.all_to_all(x, 'dp', split_axis=0, concat_axis=0, tiled=True)]
  transfers between devices with their start and end apart: 7 -> 8, of which waited for: 4 -> 6; matrix products, arithmetic and copies ran while one was open for 12% -> 1% of each run, Pallas kernels for 4% -> 19%
where the time goes in v2:
time: 189 us; the launch traced here: 186 us
  waiting for transfers between devices  55.8 us (30%)
  Pallas kernels  40.2 us (21%)
  blocking collectives  38.3 us (20%)
  starting transfers between devices  20.7 us (11%)
  local copies, waits for them, and re-layouts  14.5 us (8%)
  between operations  14.3 us (8%)
  other arithmetic  2.09 us (1%)
    all_to_all x3, waiting for transfers between devices, exchange(): return lax.all_to_all(x, 'dp', split_axis=0, concat_axis=0, tiled=True)  50.5 us
    all_to_all x1, blocking collectives, exchange(): return lax.all_to_all(x, 'dp', split_axis=0, concat_axis=0, tiled=True)  38.3 us
    pallas_call x2, Pallas kernels, terms(): pl.pallas_call(functools.partial(terms_kernel, fresh), out_shape=jax.Shap...  16.9 us
    unnamed x42, local copies, waits for them, and re-layouts  14.5 us
    all_to_all x3, starting transfers between devices, exchange(): return lax.all_to_all(x, 'dp', split_axis=0, concat_axis=0, tiled=True)  12 us
    pallas_call x2, Pallas kernels, owner(): pl.pallas_call(functools.partial(owner_kernel, len(more)), out_shape=made...  9.04 us
    pallas_call x1, Pallas kernels, pack(): pl.pallas_call(pack_kernel, out_shape=(jax.ShapeDtypeStruct((DP, ITEM_BLO...  4.06 us
    pallas_call x1, Pallas kernels, combine_last(): pl.pallas_call(last_kernel, out_shape=(jax.ShapeDtypeStruct((FRAMES, W, C...  3.89 us
  transfers between devices with their start and end apart: 8, of which 6 were waited for; matrix products, arithmetic and copies ran while one was open for 1% of the time, Pallas kernels for 19%

profile of v2, /device:TPU:16, one launch (start us, length us, event | category | flops | bytes accessed | tf_op | source)
XLA Modules:
  0.0 185.9 jit_solution(17723879212503000454)
XLA Ops:
  7.2 1.9 %collective-permute-start.1 = (bf16[4,64,256]{2,1,0:T(8,128)(2,1)}, bf16[4,64,256]{2,1,0:T(8,128)(2,1)S(1)}, u32[]{:S(2)}, u32[]{:S(2)}) collective-permute-start(bf16[4,64,256]{2,1,0:T(8,128)(2,1)} %bitcast.27), channel_id=1, source_target_pairs={{1,0},{2,1},{3,2},{4,3},{5,4},{6,5},{7,6},{9,8},{10,9},{11,10},{12... | collective-permute-start | bytes 393224 | tf_op jit(solution)/shard_map/ppermute | solution.py:509
  9.1 2.4 %collective-permute-start = (bf16[4,64,256]{2,1,0:T(8,128)(2,1)}, bf16[4,64,256]{2,1,0:T(8,128)(2,1)S(1)}, u32[]{:S(2)}, u32[]{:S(2)}) collective-permute-start(bf16[4,64,256]{2,1,0:T(8,128)(2,1)} %bitcast.28), channel_id=1, source_target_pairs={{0,1},{1,2},{2,3},{3,4},{4,5},{5,6},{6,7},{8,9},{9,10},{10,11},{11... | collective-permute-start | bytes 393224 | tf_op jit(solution)/shard_map/ppermute | solution.py:508
  11.5 0.0 copy-start.5
  11.5 0.9 copy-done.5
  12.4 0.9 copy-done.7
  13.3 0.7 copy-done.9
  14.0 0.7 copy-done.11
  14.7 0.7 copy-done.14
  15.3 1.6 route.1
  17.0 0.0 collective-permute-done.1.below
  17.0 0.0 collective-permute-done.above
  17.0 4.1 %pack.1 = (bf16[16,17,16,256]{3,2,1,0:T(8,128)(2,1)S(1)}, bf16[16,16,16,256]{3,2,1,0:T(8,128)(2,1)S(1)}) custom-call(s32[16]{0:T(128)S(1)} %get-tuple-element.32.item_slot, bf16[16,16,256]{2,1,0:T(8,128)(2,1)S(1)} %get-tuple-element.33.tags, bf16[4,16,16,256]{3,2,1,0:T(8,128)(2,1)S(1)} %get-tuple-element.34.half, ...), custom_call_target="tpu_custom_call" | custom-call | tf_op jit(solution)/shard_map/pack/pallas_call | solution.py:123
  21.1 0.0 copy-start.3
  21.1 38.3 %all_to_all.20.items = bf16[16,17,16,256]{3,2,1,0:T(8,128)(2,1)} all-to-all(bf16[16,17,16,256]{3,2,1,0:T(8,128)(2,1)S(1)} %get-tuple-element.35), channel_id=1, replica_groups=mesh['dp'=16,'tile'=8] {'dp'}, dimensions={0} | all-to-all | bytes 4456448 | tf_op jit(solution)/shard_map/all_to_all | solution.py:501
  59.4 3.7 %all-to-all-start.1 = ((bf16[16,16,16,256]{3,2,1,0:T(8,128)(2,1)}), bf16[16,16,16,256]{3,2,1,0:T(8,128)(2,1)S(1)}, u32[]{:S(2)}, u32[]{:S(2)}) async-start(bf16[16,16,16,256]{3,2,1,0:T(8,128)(2,1)} %copy-done.3), calls=%async_computation.1 | async-start | bytes 4194304 | tf_op jit(solution)/shard_map/all_to_all | solution.py:501
  63.1 1.4 convert_reduce_fusion.meta
  64.5 2.8 %item_lists.1 = (s32[28]{0:T(128)}, f32[28]{0:T(128)}, s32[7]{0:T(128)}, s32[1]{0:T(128)}, s32[28]{0:T(128)}, /*index=5*/f32[28]{0:T(128)}, s32[7]{0:T(128)}, s32[1]{0:T(128)}) custom-call(f32[16,5]{1,0:T(8,128)} %convert_reduce_fusion.meta), custom_call_target="tpu_custom_call" | custom-call | tf_op jit(solution)/shard_map/item_lists/pallas_call | solution.py:194
  67.3 0.0 copy-start.1
  67.4 1.6 copy-done.1
  69.0 2.3 %copy-done.15 = bf16[4,9,256,256]{3,2,1,0:T(8,128)(2,1)S(1)} copy-done((bf16[4,9,256,256]{3,2,1,0:T(8,128)(2,1)S(1)}, bf16[4,9,256,256]{3,2,1,0:T(8,128)(2,1)}, u32[]{:S(2)}) %copy-start.15) | copy-done | bytes 4718616
  71.3 0.7 copy-done.18
  72.0 0.7 copy-done.19
  72.6 0.7 copy-done.20
  73.3 5.2 %owner.2 = (bf16[16,3,64,256]{3,2,1,0:T(8,128)(2,1)S(1)}, bf16[16,64,256]{2,1,0:T(8,128)(2,1)S(1)}, bf16[7,256,256]{2,1,0:T(8,128)(2,1)S(1)}) custom-call(s32[28]{0:T(128)S(1)} %copy-done.18, f32[28]{0:T(128)S(1)} %copy-done.20, s32[7]{0:T(128)S(1)} %copy-done.19, s32[1]{0:T(128)} %get-tuple-element.46.groups, bf16[16,17,16,256]{3,2,1,0:T(8,128)(2,1)S(1)} %copy-done.1, ...), custom_call_target="tpu_custom_call" | custom-call | flops 8000000000 | bytes 16000000 | tf_op jit(solution)/shard_map/owner/pallas_call | solution.py:300
  78.5 7.8 %first_terms.1.refs_0_ = f32[8,4,9,32,256]{4,3,2,1,0:T(8,128)} custom-call(s32[28]{0:T(128)S(1)} %copy-done.18, s32[7]{0:T(128)S(1)} %copy-done.19, s32[1]{0:T(128)} %get-tuple-element.46.groups, bf16[16,17,16,256]{3,2,1,0:T(8,128)(2,1)S(1)} %copy-done.2, bf16[7,256,256]{2,1,0:T(8,128)(2,1)S(1)} %get-tuple-element.51.grads), custom_call_target="tpu_custom_call" | custom-call | flops 4000000000 | bytes 15000000 | tf_op jit(solution)/shard_map/first_terms/pallas_call | solution.py:405
  86.3 8.5 %all-to-all-done.1.items = bf16[16,16,16,256]{3,2,1,0:T(8,128)(2,1)S(1)} async-done(((bf16[16,16,16,256]{3,2,1,0:T(8,128)(2,1)}), bf16[16,16,16,256]{3,2,1,0:T(8,128)(2,1)S(1)}, u32[]{:S(2)}, u32[]{:S(2)}) %all-to-all-start.1) | async-done | bytes 2097184 | tf_op jit(solution)/shard_map/all_to_all | solution.py:501
  94.8 4.4 %all-to-all-start.3 = ((bf16[16,3,64,256]{3,2,1,0:T(8,128)(2,1)}), bf16[16,3,64,256]{3,2,1,0:T(8,128)(2,1)}, u32[]{:S(2)}, u32[]{:S(2)}) async-start(bf16[16,3,64,256]{3,2,1,0:T(8,128)(2,1)} %copy-done.4), calls=%async_computation.3 | async-start | bytes 3145728 | tf_op jit(solution)/shard_map/all_to_all | solution.py:501
  99.2 0.0 reduce-scatter.2.cloned.1.call-start
  99.3 0.0 copy-start.16
  99.3 2.3 %copy-done.16 = bf16[4,9,256,256]{3,2,1,0:T(8,128)(2,1)S(1)} copy-done((bf16[4,9,256,256]{3,2,1,0:T(8,128)(2,1)S(1)}, bf16[4,9,256,256]{3,2,1,0:T(8,128)(2,1)}, u32[]{:S(2)}) %copy-start.16) | copy-done | bytes 4718616
  101.6 3.8 %owner.3 = (bf16[16,5,64,256]{3,2,1,0:T(8,128)(2,1)S(1)}, bf16[7,256,256]{2,1,0:T(8,128)(2,1)S(1)}) custom-call(s32[28]{0:T(128)S(1)} %copy-done.12, f32[28]{0:T(128)S(1)} %copy-done.17, s32[7]{0:T(128)S(1)} %copy-done.13, s32[1]{0:T(128)} %get-tuple-element.41.groups, bf16[16,16,16,256]{3,2,1,0:T(8,128)(2,1)S(1)} %all-to-all-done.1.items, ...), custom_call_target="tpu_custom_call" | custom-call | flops 8000000000 | bytes 16000000 | tf_op jit(solution)/shard_map/owner/pallas_call | solution.py:300
  105.5 1.5 copy-done
  107.0 9.1 %last_terms.1 = f32[8,4,9,32,256]{4,3,2,1,0:T(8,128)} custom-call(s32[28]{0:T(128)S(1)} %copy-done.12, s32[7]{0:T(128)S(1)} %copy-done.13, s32[1]{0:T(128)} %get-tuple-element.41.groups, bf16[16,16,16,256]{3,2,1,0:T(8,128)(2,1)S(1)} %all-to-all-done.1.items, bf16[7,256,256]{2,1,0:T(8,128)(2,1)S(1)} %get-tuple-element.49.grads, ...), custom_call_target="tpu_custom_call" | custom-call | flops 4000000000 | bytes 15000000 | tf_op jit(solution)/shard_map/last_terms/pallas_call | solution.py:405
  116.1 5.4 %all-to-all-done.3.got = bf16[16,3,64,256]{3,2,1,0:T(8,128)(2,1)} async-done(((bf16[16,3,64,256]{3,2,1,0:T(8,128)(2,1)}), bf16[16,3,64,256]{3,2,1,0:T(8,128)(2,1)}, u32[]{:S(2)}, u32[]{:S(2)}) %all-to-all-start.3) | async-done | bytes 1572896 | tf_op jit(solution)/shard_map/all_to_all | solution.py:501
  121.6 0.0 reduce-scatter.2.cloned.1.call-update
  121.6 0.0 copy-start.6
  121.6 3.9 %all-to-all-start.2 = ((bf16[16,5,64,256]{3,2,1,0:T(8,128)(2,1)}), bf16[16,5,64,256]{3,2,1,0:T(8,128)(2,1)S(1)}, u32[]{:S(2)}, u32[]{:S(2)}) async-start(bf16[16,5,64,256]{3,2,1,0:T(8,128)(2,1)} %copy-done), calls=%async_computation.2 | async-start | bytes 5242880 | tf_op jit(solution)/shard_map/all_to_all | solution.py:501
  125.5 0.0 copy-start.10
  125.5 1.8 combine_first.1.so_far
  127.3 36.6 %all-to-all-done.2.got = bf16[16,5,64,256]{3,2,1,0:T(8,128)(2,1)S(1)} async-done(((bf16[16,5,64,256]{3,2,1,0:T(8,128)(2,1)}), bf16[16,5,64,256]{3,2,1,0:T(8,128)(2,1)S(1)}, u32[]{:S(2)}, u32[]{:S(2)}) %all-to-all-start.2) | async-done | bytes 2621472 | tf_op jit(solution)/shard_map/all_to_all | solution.py:501
  164.0 0.9 copy-done.8
  164.9 3.9 %combine_last.1 = (bf16[4,64,256]{2,1,0:T(8,128)(2,1)}, f32[4,64,256]{2,1,0:T(8,128)S(1)}, bf16[2,4,64,256]{3,2,1,0:T(8,128)(2,1)S(1)}, f32[4,4]{1,0:T(4,128)}) custom-call(s32[16]{0:T(128)S(1)} %get-tuple-element.32.item_slot, f32[4,4]{1,0:T(4,128)S(1)} %bitcast.32, bf16[16,5,64,256]{3,2,1,0:T(8,128)(2,1)S(1)} %all-to-all-done.2.got, ...), custom_call_target="tpu_custom_call" | custom-call | tf_op jit(solution)/shard_map/combine_last/pallas_call | solution.py:477
  168.8 1.9 %collective-permute-start.2 = (bf16[4,64,256]{2,1,0:T(8,128)(2,1)S(1)}, bf16[4,64,256]{2,1,0:T(8,128)(2,1)S(1)}, u32[]{:S(2)}, u32[]{:S(2)}) collective-permute-start(bf16[4,64,256]{2,1,0:T(8,128)(2,1)S(1)} %get-tuple-element.64), channel_id=1, source_target_pairs={{1,0},{2,1},{3,2},{4,3},{5,4},{6,5},{7,6},{9,8},{10,9},{11,10},{12... | collective-permute-start | bytes 393224 | tf_op jit(solution)/shard_map/ppermute | solution.py:534
  170.7 2.4 %collective-permute-start.3 = (bf16[4,64,256]{2,1,0:T(8,128)(2,1)S(1)}, bf16[4,64,256]{2,1,0:T(8,128)(2,1)S(1)}, u32[]{:S(2)}, u32[]{:S(2)}) collective-permute-start(bf16[4,64,256]{2,1,0:T(8,128)(2,1)S(1)} %get-tuple-element.65), channel_id=1, source_target_pairs={{0,1},{1,2},{2,3},{3,4},{4,5},{5,6},{6,7},{8,9},{9,10},{10,11},{11... | collective-permute-start | bytes 393224 | tf_op jit(solution)/shard_map/ppermute | solution.py:535
  173.2 1.5 collective-permute-done.2
  174.7 3.4 %collective-permute-done.3 = bf16[4,64,256]{2,1,0:T(8,128)(2,1)S(1)} collective-permute-done((bf16[4,64,256]{2,1,0:T(8,128)(2,1)S(1)}, bf16[4,64,256]{2,1,0:T(8,128)(2,1)S(1)}, u32[]{:S(2)}, u32[]{:S(2)}) %collective-permute-start.3) | collective-permute-done | bytes 131104 | tf_op jit(solution)/shard_map/ppermute | solution.py:535
  178.1 0.7 fusion
  178.8 0.3 reduce-scatter.2.cloned.1.call-done
  (24 shorter events, 0.1 us)
Async XLA Ops:
  7.2 9.8 %collective-permute-start.1 = (bf16[4,64,256]{2,1,0:T(8,128)(2,1)}, bf16[4,64,256]{2,1,0:T(8,128)(2,1)S(1)}, u32[]{:S(2)}, u32[]{:S(2)}) collective-permute-start(bf16[4,64,256]{2,1,0:T(8,128)(2,1)} %bitcast.27), channel_id=1, source_target_pairs={{1,0},{2,1},{3,2},{4,3},{5,4},{6,5},{7,6},{9,8},{10,9},{11,10},{12... | collective-permute-start | bytes 393224 | tf_op jit(solution)/shard_map/ppermute | solution.py:509
  9.1 7.9 %collective-permute-start = (bf16[4,64,256]{2,1,0:T(8,128)(2,1)}, bf16[4,64,256]{2,1,0:T(8,128)(2,1)S(1)}, u32[]{:S(2)}, u32[]{:S(2)}) collective-permute-start(bf16[4,64,256]{2,1,0:T(8,128)(2,1)} %bitcast.28), channel_id=1, source_target_pairs={{0,1},{1,2},{2,3},{3,4},{4,5},{5,6},{6,7},{8,9},{9,10},{10,11},{11... | collective-permute-start | bytes 393224 | tf_op jit(solution)/shard_map/ppermute | solution.py:508
  11.5 0.9 copy-start.5
  12.4 0.9 copy-start.7
  13.3 0.7 copy-start.9
  14.0 0.7 copy-start.11
  14.7 0.7 copy-start.14
  21.1 38.4 %copy-start.3 = (bf16[16,16,16,256]{3,2,1,0:T(8,128)(2,1)}, bf16[16,16,16,256]{3,2,1,0:T(8,128)(2,1)S(1)}, u32[]{:S(2)}) copy-start(bf16[16,16,16,256]{3,2,1,0:T(8,128)(2,1)S(1)} %get-tuple-element.42) | copy-start | bytes 6291460
  59.4 35.4 %all-to-all-start.1 = ((bf16[16,16,16,256]{3,2,1,0:T(8,128)(2,1)}), bf16[16,16,16,256]{3,2,1,0:T(8,128)(2,1)S(1)}, u32[]{:S(2)}, u32[]{:S(2)}) async-start(bf16[16,16,16,256]{3,2,1,0:T(8,128)(2,1)} %copy-done.3), calls=%async_computation.1 | async-start | bytes 4194304 | tf_op jit(solution)/shard_map/all_to_all | solution.py:501
  67.3 1.6 copy-start.1
  69.0 2.3 %copy-start.15 = (bf16[4,9,256,256]{3,2,1,0:T(8,128)(2,1)S(1)}, bf16[4,9,256,256]{3,2,1,0:T(8,128)(2,1)}, u32[]{:S(2)}) copy-start(bf16[4,9,256,256]{3,2,1,0:T(8,128)(2,1)} %param.7) | copy-start | bytes 14155780
  71.3 0.7 copy-start.18
  72.0 0.7 copy-start.19
  72.6 0.7 copy-start.20
  73.3 5.2 %copy-start.2 = (bf16[16,17,16,256]{3,2,1,0:T(8,128)(2,1)S(1)}, bf16[16,17,16,256]{3,2,1,0:T(8,128)(2,1)}, u32[]{:S(2)}) copy-start(bf16[16,17,16,256]{3,2,1,0:T(8,128)(2,1)} %all_to_all.20.items) | copy-start | bytes 6684676
  78.5 7.8 %copy-start.4 = (bf16[16,3,64,256]{3,2,1,0:T(8,128)(2,1)}, bf16[16,3,64,256]{3,2,1,0:T(8,128)(2,1)S(1)}, u32[]{:S(2)}) copy-start(bf16[16,3,64,256]{3,2,1,0:T(8,128)(2,1)S(1)} %get-tuple-element.53) | copy-start | bytes 4718596
  86.3 13.0 %copy-start.12 = (s32[28]{0:T(128)S(1)}, s32[28]{0:T(128)}, u32[]{:S(2)}) copy-start(s32[28]{0:T(128)} %get-tuple-element.38.order) | copy-start | bytes 340
  86.3 13.0 %copy-start.13 = (s32[7]{0:T(128)S(1)}, s32[7]{0:T(128)}, u32[]{:S(2)}) copy-start(s32[7]{0:T(128)} %get-tuple-element.40.group_expert) | copy-start | bytes 88
  86.3 13.0 %copy-start.17 = (f32[28]{0:T(128)S(1)}, f32[28]{0:T(128)}, u32[]{:S(2)}) copy-start(f32[28]{0:T(128)} %get-tuple-element.39.scale) | copy-start | bytes 340
  94.8 26.8 %all-to-all-start.3 = ((bf16[16,3,64,256]{3,2,1,0:T(8,128)(2,1)}), bf16[16,3,64,256]{3,2,1,0:T(8,128)(2,1)}, u32[]{:S(2)}, u32[]{:S(2)}) async-start(bf16[16,3,64,256]{3,2,1,0:T(8,128)(2,1)} %copy-done.4), calls=%async_computation.3 | async-start | bytes 3145728 | tf_op jit(solution)/shard_map/all_to_all | solution.py:501
  99.2 79.9 %reduce-scatter.2.cloned.1.call-start = ((), (), s32[]{:S(2)}) async-start(), calls=%async_computation.5 | async-start | bytes 10616832 | tf_op jit(solution)/shard_map/reduce_scatter | solution.py:526
  99.3 2.3 %copy-start.16 = (bf16[4,9,256,256]{3,2,1,0:T(8,128)(2,1)S(1)}, bf16[4,9,256,256]{3,2,1,0:T(8,128)(2,1)}, u32[]{:S(2)}) copy-start(bf16[4,9,256,256]{3,2,1,0:T(8,128)(2,1)} %param.7) | copy-start | bytes 14155780
  105.5 1.5 copy-start
  121.6 3.9 %copy-start.6 = (bf16[4,1,64,256]{3,2,1,0:T(8,128)(2,1)S(1)}, bf16[4,1,64,256]{3,2,1,0:T(8,128)(2,1)}, u32[]{:S(2)}) copy-start(bf16[4,1,64,256]{3,2,1,0:T(8,128)(2,1)} %param.11) | copy-start | bytes 393220
  121.6 42.4 %all-to-all-start.2 = ((bf16[16,5,64,256]{3,2,1,0:T(8,128)(2,1)}), bf16[16,5,64,256]{3,2,1,0:T(8,128)(2,1)S(1)}, u32[]{:S(2)}, u32[]{:S(2)}) async-start(bf16[16,5,64,256]{3,2,1,0:T(8,128)(2,1)} %copy-done), calls=%async_computation.2 | async-start | bytes 5242880 | tf_op jit(solution)/shard_map/all_to_all | solution.py:501
  125.5 38.5 %copy-start.10 = (f32[4,1,4]{2,1,0:T(1,128)S(1)}, f32[4,1,4]{2,1,0:T(1,128)}, u32[]{:S(2)}) copy-start(f32[4,1,4]{2,1,0:T(1,128)} %param.10) | copy-start | bytes 196
  164.0 0.9 copy-start.8
  168.8 5.9 %collective-permute-start.2 = (bf16[4,64,256]{2,1,0:T(8,128)(2,1)S(1)}, bf16[4,64,256]{2,1,0:T(8,128)(2,1)S(1)}, u32[]{:S(2)}, u32[]{:S(2)}) collective-permute-start(bf16[4,64,256]{2,1,0:T(8,128)(2,1)S(1)} %get-tuple-element.64), channel_id=1, source_target_pairs={{1,0},{2,1},{3,2},{4,3},{5,4},{6,5},{7,6},{9,8},{10,9},{11,10},{12... | collective-permute-start | bytes 393224 | tf_op jit(solution)/shard_map/ppermute | solution.py:534
  170.7 7.3 %collective-permute-start.3 = (bf16[4,64,256]{2,1,0:T(8,128)(2,1)S(1)}, bf16[4,64,256]{2,1,0:T(8,128)(2,1)S(1)}, u32[]{:S(2)}, u32[]{:S(2)}) collective-permute-start(bf16[4,64,256]{2,1,0:T(8,128)(2,1)S(1)} %get-tuple-element.65), channel_id=1, source_target_pairs={{0,1},{1,2},{2,3},{3,4},{4,5},{5,6},{6,7},{8,9},{9,10},{10,11},{11... | collective-permute-start | bytes 393224 | tf_op jit(solution)/shard_map/ppermute | solution.py:535
Sparse Core Ops, SparseCore 0:
  121.7 57.3 reduce-scatter.1
